TPU v7x, 128 devices: a whole 4x4x4 slice. The times are simulated.
128 devices in a mesh: ctx: 8 (over z_lo, x), fsdp: 16 (over y, z_hi, core).
Axes of the slice: x: 4, y: 4, z: 4 (z_hi: 2, z_lo: 2; z = z_hi * 2 + z_lo), core: 2. Of those that a mesh axis runs over, the one named last changes fastest.
Arguments:
- inputs: bfloat16 [16, 1024, 1152], P('fsdp', 'ctx'), may hold values from -6 to 6
- pair_order: int32 [16, 8], P('fsdp'), may hold values from 0 to 7, each once within a row
- attn_gain: bfloat16 [1152], P(('ctx', 'fsdp')), may hold values from 0.099609375 to 1.8984375
- query_gain: bfloat16 [256], P(('ctx', 'fsdp')), may hold values from 0.099609375 to 1.8984375
- key_gain: bfloat16 [256], P(('ctx', 'fsdp')), may hold values from 0.099609375 to 1.8984375
- mixer_gain: bfloat16 [1152], P(('ctx', 'fsdp')), may hold values from 0.099609375 to 1.8984375
- ffn_gain: bfloat16 [1152], P(('ctx', 'fsdp')), may hold values from 0.099609375 to 1.8984375
- branch_gain: bfloat16 [1152], P(('ctx', 'fsdp')), may hold values from 0.099609375 to 1.8984375
- query_weight: bfloat16 [1152, 1024], P(('ctx', 'fsdp')), may hold values from -0.1875 to 0.1875
- key_weight: bfloat16 [1152, 256], P(('ctx', 'fsdp')), may hold values from -0.1875 to 0.1875
- value_weight: bfloat16 [1152, 256], P(('ctx', 'fsdp')), may hold values from -0.1875 to 0.1875
- output_weight: bfloat16 [1024, 1152], P(('ctx', 'fsdp')), may hold values from -0.1875 to 0.1875
- gate_weight: bfloat16 [1152, 6912], P('ctx', 'fsdp'), may hold values from -0.1875 to 0.1875
- up_weight: bfloat16 [1152, 6912], P('ctx', 'fsdp'), may hold values from -0.1875 to 0.1875
- down_weight: bfloat16 [6912, 1152], P('fsdp', 'ctx'), may hold values from -0.078125 to 0.078125
- cotangent: bfloat16 [16, 1024, 1152], P('fsdp', 'ctx'), may hold values from -6 to 6
Outputs:
- outputs: float32 [16, 1024, 1152], P('fsdp', 'ctx')
- inputs_grad: float32 [16, 1024, 1152], P('fsdp', 'ctx')
- attn_gain_grad: float32 [1152], P(('ctx', 'fsdp'))
- query_gain_grad: float32 [256], P(('ctx', 'fsdp'))
- key_gain_grad: float32 [256], P(('ctx', 'fsdp'))
- mixer_gain_grad: float32 [1152], P(('ctx', 'fsdp'))
- ffn_gain_grad: float32 [1152], P(('ctx', 'fsdp'))
- branch_gain_grad: float32 [1152], P(('ctx', 'fsdp'))
- query_weight_grad: float32 [1152, 1024], P(('ctx', 'fsdp'))
- key_weight_grad: float32 [1152, 256], P(('ctx', 'fsdp'))
- value_weight_grad: float32 [1152, 256], P(('ctx', 'fsdp'))
- output_weight_grad: float32 [1024, 1152], P(('ctx', 'fsdp'))
- gate_weight_grad: float32 [1152, 6912], P('ctx', 'fsdp')
- up_weight_grad: float32 [1152, 6912], P('ctx', 'fsdp')
- down_weight_grad: float32 [6912, 1152], P('fsdp', 'ctx')
Inputs may be any that keep to these rules, and one draw needn't show every extreme that they name: Each row of pair_order names every number of 0 to 7 once.
All inputs are finite; a program needn't handle non-finite values.
Results may differ from a plain program's by a relative error of at most 0.04.
Values may be sent and summed in bfloat16 or wider, within the bound.
A program may use at most 128 MiB of HBM per device.

v0:
```python
from functools import partial

import jax
import jax.numpy as jnp
from jax import lax
from jax.sharding import PartitionSpec as P

EPS = 1e-06
SCALE = 0.0625
BASE = 1000000.0
MASKED = -1e30


def rms_norm(values, gain):
    return values * lax.rsqrt(jnp.mean(values * values, axis=-1, keepdims=True) + EPS) * gain


def rotary(values, cosines, sines):
    half = values.shape[-1] // 2
    first = values[..., :half]
    second = values[..., half:]
    return jnp.concatenate(
        [first * cosines - second * sines, second * cosines + first * sines], axis=-1
    )


def angles(positions, width):
    half = width // 2
    freqs = BASE ** (-jnp.arange(half, dtype=jnp.float32) / half)
    return positions.astype(jnp.float32)[:, None] * freqs[None, :]


def token_positions(pairs, tok_rows):
    half = tok_rows // 2
    index = jnp.arange(tok_rows, dtype=jnp.int32)
    count = 2 * pairs.shape[0]
    blocks = jnp.where(index[None, :] < half, pairs[:, None], count - 1 - pairs[:, None])
    return blocks * half + index[None, :] % half


def matmul(left, right):
    return jnp.dot(left, right, preferred_element_type=jnp.float32)


def matmul_tn(left, right):
    return lax.dot_general(
        left, right, (((0,), (0,)), ((), ())), preferred_element_type=jnp.float32
    )


def matmul_nt(left, right):
    return lax.dot_general(
        left, right, (((1,), (1,)), ((), ())), preferred_element_type=jnp.float32
    )


def score_block(query_low, key_all, causal):
    scores = (
        jnp.einsum("thd,kd->htk", query_low, key_all, preferred_element_type=jnp.float32) * SCALE
    )
    return jnp.where(causal[None], scores, MASKED)


def ffn_front(tokens_all, gate_all, up_all):
    gate_pre = matmul(tokens_all, gate_all)
    up_pre = matmul(tokens_all, up_all)
    activated, gelu_back = jax.vjp(partial(jax.nn.gelu, approximate=True), gate_pre)
    hidden_low = (activated * up_pre).astype(jnp.bfloat16)
    return (up_pre, activated, gelu_back, hidden_low)


def body(
    inputs,
    pair_order,
    attn_gain,
    query_gain,
    key_gain,
    mixer_gain,
    ffn_gain,
    branch_gain,
    query_weight,
    key_weight,
    value_weight,
    output_weight,
    gate_weight,
    up_weight,
    down_weight,
    cotangent,
):
    gathered = (
        lax.all_gather(attn_gain, ("ctx", "fsdp"), axis=0, tiled=True),
        lax.all_gather(query_gain, ("ctx", "fsdp"), axis=0, tiled=True),
        lax.all_gather(key_gain, ("ctx", "fsdp"), axis=0, tiled=True),
        lax.all_gather(mixer_gain, ("ctx", "fsdp"), axis=0, tiled=True),
        lax.all_gather(ffn_gain, ("ctx", "fsdp"), axis=0, tiled=True),
        lax.all_gather(branch_gain, ("ctx", "fsdp"), axis=0, tiled=True),
        lax.all_gather(query_weight, ("ctx", "fsdp"), axis=0, tiled=True),
        lax.all_gather(key_weight, ("ctx", "fsdp"), axis=0, tiled=True),
        lax.all_gather(value_weight, ("ctx", "fsdp"), axis=0, tiled=True),
        lax.all_gather(output_weight, ("ctx", "fsdp"), axis=0, tiled=True),
    )
    gain_in = gathered[0].astype(jnp.float32)
    gain_query = gathered[1].astype(jnp.float32)
    gain_key = gathered[2].astype(jnp.float32)
    gain_mixed = gathered[3].astype(jnp.float32)
    gain_ffn = gathered[4].astype(jnp.float32)
    gain_branch = gathered[5].astype(jnp.float32)
    query_all_w = gathered[6]
    key_all_w = gathered[7]
    value_all_w = gathered[8]
    output_all_w = gathered[9]
    gate_all, up_all, down_all = (
        lax.all_gather(gate_weight, "ctx", axis=0, tiled=True),
        lax.all_gather(up_weight, "ctx", axis=0, tiled=True),
        lax.all_gather(down_weight, "ctx", axis=1, tiled=True),
    )
    rows = inputs.shape[1]
    head_dim = key_weight.shape[1]
    heads = query_weight.shape[1] // head_dim
    slot = lax.axis_index("ctx")
    all_positions = token_positions(pair_order[0], rows).reshape(-1)
    own_positions = lax.dynamic_slice_in_dim(all_positions, slot * rows, rows)
    angle = angles(own_positions, head_dim)
    cosines = jnp.cos(angle)
    sines = jnp.sin(angle)
    causal = all_positions[None, :] <= own_positions[:, None]
    hidden_in = inputs[0].astype(jnp.float32)
    normed_in, norm_in_back = jax.vjp(rms_norm, hidden_in, gain_in)
    attn_input = normed_in.astype(jnp.bfloat16)
    queries_raw = matmul(attn_input, query_all_w)
    keys_raw = matmul(attn_input, key_all_w)
    values_raw = matmul(attn_input, value_all_w)

    def query_shape(raw, gain):
        return rotary(
            rms_norm(raw.reshape(rows, heads, head_dim), gain),
            cosines[:, None, :],
            sines[:, None, :],
        )

    def key_shape(raw, gain):
        return rotary(rms_norm(raw, gain), cosines, sines)

    queries_rot, query_back = jax.vjp(query_shape, queries_raw, gain_query)
    keys_rot, key_back = jax.vjp(key_shape, keys_raw, gain_key)
    query_low = queries_rot.astype(jnp.bfloat16)
    key_low = keys_rot.astype(jnp.bfloat16)
    value_low = values_raw.astype(jnp.bfloat16)
    key_all, value_all = (
        lax.all_gather(key_low, "ctx", axis=0, tiled=True),
        lax.all_gather(value_low, "ctx", axis=0, tiled=True),
    )
    scores = score_block(query_low, key_all, causal)
    peak = jnp.max(scores, axis=-1, keepdims=True)
    expo = jnp.exp(scores - peak)
    total = jnp.sum(expo, axis=-1, keepdims=True)
    probs = expo / total
    log_total = peak + jnp.log(total)
    probs_low = probs.astype(jnp.bfloat16)
    mixed = jnp.einsum("htk,kd->thd", probs_low, value_all, preferred_element_type=jnp.float32)
    mixed_low = mixed.reshape(rows, heads * head_dim).astype(jnp.bfloat16)
    attn_out = matmul(mixed_low, output_all_w)
    post_attn, post_attn_back = jax.vjp(rms_norm, attn_out, gain_mixed)
    resid = hidden_in + post_attn
    normed_mid, mid_back = jax.vjp(rms_norm, resid, gain_ffn)
    ffn_input = normed_mid.astype(jnp.bfloat16)
    tokens_all = lax.all_gather(ffn_input, "fsdp", axis=0, tiled=True)
    up_pre, activated, gelu_back, hidden_low = ffn_front(tokens_all, gate_all, up_all)
    partial_out = matmul(hidden_low, down_all)
    branch_raw = lax.psum_scatter(partial_out, "fsdp", scatter_dimension=0, tiled=True)
    post_ffn, post_ffn_back = jax.vjp(rms_norm, branch_raw, gain_branch)
    outputs = (resid + post_ffn)[None]
    upstream = cotangent[0].astype(jnp.float32)
    grad_branch, grad_gain_branch = post_ffn_back(upstream)
    branch_low = grad_branch.astype(jnp.bfloat16)
    branch_all = lax.all_gather(branch_low, "fsdp", axis=0, tiled=True)
    grad_hidden = matmul_nt(branch_all, down_all)
    grad_down = matmul_tn(hidden_low, branch_all)
    grad_gate_pre = gelu_back(grad_hidden * up_pre)[0]
    gate_low = grad_gate_pre.astype(jnp.bfloat16)
    up_low = (grad_hidden * activated).astype(jnp.bfloat16)
    grad_tokens_all = matmul_nt(gate_low, gate_all) + matmul_nt(up_low, up_all)
    grad_gate = matmul_tn(tokens_all, gate_low)
    grad_up = matmul_tn(tokens_all, up_low)
    grad_ffn_input = lax.psum_scatter(grad_tokens_all, "fsdp", scatter_dimension=0, tiled=True)
    gate_grad, up_grad, down_grad = (
        lax.psum_scatter(grad_gate, "ctx", scatter_dimension=0, tiled=True),
        lax.psum_scatter(grad_up, "ctx", scatter_dimension=0, tiled=True),
        lax.psum_scatter(grad_down, "ctx", scatter_dimension=1, tiled=True),
    )
    grad_resid_mid, grad_gain_ffn = mid_back(grad_ffn_input)
    grad_resid = upstream + grad_resid_mid
    grad_attn_out, grad_gain_mixed = post_attn_back(grad_resid)
    attn_low = grad_attn_out.astype(jnp.bfloat16)
    query_back_w, key_back_w, value_back_w, output_back_w = (
        lax.all_gather(query_weight, ("ctx", "fsdp"), axis=0, tiled=True),
        lax.all_gather(key_weight, ("ctx", "fsdp"), axis=0, tiled=True),
        lax.all_gather(value_weight, ("ctx", "fsdp"), axis=0, tiled=True),
        lax.all_gather(output_weight, ("ctx", "fsdp"), axis=0, tiled=True),
    )
    grad_mixed = matmul_nt(attn_low, output_back_w)
    grad_output_w = matmul_tn(mixed_low, attn_low)
    mixed_grad_low = grad_mixed.astype(jnp.bfloat16).reshape(rows, heads, head_dim)
    scores_again = score_block(query_low, key_all, causal)
    probs_again = jnp.exp(scores_again - log_total)
    probs_again_low = probs_again.astype(jnp.bfloat16)
    grad_value_all = jnp.einsum(
        "htk,thd->kd", probs_again_low, mixed_grad_low, preferred_element_type=jnp.float32
    )
    grad_probs = jnp.einsum(
        "thd,kd->htk", mixed_grad_low, value_all, preferred_element_type=jnp.float32
    )
    delta = jnp.sum(grad_probs * probs_again, axis=-1, keepdims=True)
    grad_scores_low = (probs_again * (grad_probs - delta)).astype(jnp.bfloat16)
    grad_query_rot = (
        jnp.einsum("htk,kd->thd", grad_scores_low, key_all, preferred_element_type=jnp.float32)
        * SCALE
    )
    grad_key_all = (
        jnp.einsum("htk,thd->kd", grad_scores_low, query_low, preferred_element_type=jnp.float32)
        * SCALE
    )
    grad_key_rot, grad_value = (
        lax.psum_scatter(grad_key_all, "ctx", scatter_dimension=0, tiled=True),
        lax.psum_scatter(grad_value_all, "ctx", scatter_dimension=0, tiled=True),
    )
    grad_query_raw, grad_gain_query = query_back(grad_query_rot)
    grad_key_raw, grad_gain_key = key_back(grad_key_rot)
    query_glow = grad_query_raw.astype(jnp.bfloat16)
    key_glow = grad_key_raw.astype(jnp.bfloat16)
    value_glow = grad_value.astype(jnp.bfloat16)
    grad_attn_input = (
        matmul_nt(query_glow, query_back_w)
        + matmul_nt(key_glow, key_back_w)
        + matmul_nt(value_glow, value_back_w)
    )
    grad_query_w = matmul_tn(attn_input, query_glow)
    grad_key_w = matmul_tn(attn_input, key_glow)
    grad_value_w = matmul_tn(attn_input, value_glow)
    grad_hidden_in, grad_gain_in = norm_in_back(grad_attn_input)
    inputs_grad = (grad_resid + grad_hidden_in)[None]
    summed = (
        lax.psum_scatter(grad_gain_in, ("ctx", "fsdp"), scatter_dimension=0, tiled=True),
        lax.psum_scatter(grad_gain_query, ("ctx", "fsdp"), scatter_dimension=0, tiled=True),
        lax.psum_scatter(grad_gain_key, ("ctx", "fsdp"), scatter_dimension=0, tiled=True),
        lax.psum_scatter(grad_gain_mixed, ("ctx", "fsdp"), scatter_dimension=0, tiled=True),
        lax.psum_scatter(grad_gain_ffn, ("ctx", "fsdp"), scatter_dimension=0, tiled=True),
        lax.psum_scatter(grad_gain_branch, ("ctx", "fsdp"), scatter_dimension=0, tiled=True),
        lax.psum_scatter(grad_query_w, ("ctx", "fsdp"), scatter_dimension=0, tiled=True),
        lax.psum_scatter(grad_key_w, ("ctx", "fsdp"), scatter_dimension=0, tiled=True),
        lax.psum_scatter(grad_value_w, ("ctx", "fsdp"), scatter_dimension=0, tiled=True),
        lax.psum_scatter(grad_output_w, ("ctx", "fsdp"), scatter_dimension=0, tiled=True),
    )
    return (
        outputs,
        inputs_grad,
        summed[0],
        summed[1],
        summed[2],
        summed[3],
        summed[4],
        summed[5],
        summed[6],
        summed[7],
        summed[8],
        summed[9],
        gate_grad,
        up_grad,
        down_grad,
    )


def solution(mesh):
    placed = (
        P("fsdp", "ctx", None),
        P("fsdp", None),
        P(("ctx", "fsdp")),
        P(("ctx", "fsdp")),
        P(("ctx", "fsdp")),
        P(("ctx", "fsdp")),
        P(("ctx", "fsdp")),
        P(("ctx", "fsdp")),
        P(("ctx", "fsdp"), None),
        P(("ctx", "fsdp"), None),
        P(("ctx", "fsdp"), None),
        P(("ctx", "fsdp"), None),
        P("ctx", "fsdp"),
        P("ctx", "fsdp"),
        P("fsdp", "ctx"),
        P("fsdp", "ctx", None),
    )
    return jax.shard_map(
        body,
        mesh=mesh,
        in_specs=placed,
        out_specs=(
            P("fsdp", "ctx", None),
            P("fsdp", "ctx", None),
            P(("ctx", "fsdp")),
            P(("ctx", "fsdp")),
            P(("ctx", "fsdp")),
            P(("ctx", "fsdp")),
            P(("ctx", "fsdp")),
            P(("ctx", "fsdp")),
            P(("ctx", "fsdp"), None),
            P(("ctx", "fsdp"), None),
            P(("ctx", "fsdp"), None),
            P(("ctx", "fsdp"), None),
            P("ctx", "fsdp"),
            P("ctx", "fsdp"),
            P("fsdp", "ctx"),
        ),
        check_vma=False,
    )
```

profile of v0, /device:TPU:0, one launch (start us, length us, event | category | flops | bytes accessed | tf_op | source)
XLA Modules:
  0.0 1319.2 jit_solution(13563703864757151820)
XLA Ops:
  14.5 68.7 %all-reduce.22 = (bf16[1152]{0:T(1024)(128)(2,1)S(1)}, bf16[256]{0:T(256)(128)(2,1)S(1)}, bf16[256]{0:T(256)(128)(2,1)S(1)}, bf16[1152]{0:T(1024)(128)(2,1)S(1)}...) all-reduce(bf16[1152]{0:T(1024)(128)(2,1)S(1)} %dynamic-update-slic, ...), channel_id=1, replica_groups=mesh['ctx'=8,'fsdp'=16] {'ctx','fsdp'}, use_global_device_ids=true, to_apply=%add.4 | all-reduce | flops 5120 | bytes 20480
  83.2 175.8 %all-gather.1 = bf16[128,9,256]{2,1,0:T(8,128)(2,1)S(1)} all-gather(bf16[1,9,256]{2,1,0:T(8,128)(2,1)} %bitcast.157), channel_id=1, replica_groups=mesh['ctx'=8,'fsdp'=16] {'ctx','fsdp'}, dimensions={0}, use_global_device_ids=true | all-gather | bytes 594432 | tf_op jit(solution)/shard_map/all_gather | solution.py:98
  259.3 173.8 %all-gather = bf16[128,9,256]{2,1,0:T(8,128)(2,1)S(1)} all-gather(bf16[1,9,256]{2,1,0:T(8,128)(2,1)S(1)} %bitcast.158), channel_id=1, replica_groups=mesh['ctx'=8,'fsdp'=16] {'ctx','fsdp'}, dimensions={0}, use_global_device_ids=true | all-gather | bytes 594432 | tf_op jit(solution)/shard_map/all_gather | solution.py:99
  435.8 28.9 %all_gather.60 = bf16[1024,256]{1,0:T(8,128)(2,1)S(1)} all-gather(bf16[128,256]{1,0:T(8,128)(2,1)S(1)} %pad_maximum_fusion.3), channel_id=1, replica_groups=mesh['ctx'=8,'fsdp'=16] {'ctx'}, dimensions={0}, use_global_device_ids=true | all-gather | bytes 589824 | tf_op jit(solution)/shard_map/all_gather | solution.py:150
  465.0 31.1 %all_gather.57 = bf16[1024,256]{1,0:T(8,128)(2,1)} all-gather(bf16[128,256]{1,0:T(8,128)(2,1)S(1)} %convolution_convert_fusion.2), channel_id=1, replica_groups=mesh['ctx'=8,'fsdp'=16] {'ctx'}, dimensions={0}, use_global_device_ids=true | all-gather | bytes 589824 | tf_op jit(solution)/shard_map/all_gather | solution.py:151
  512.3 33.1 %all_gather.67 = bf16[1152,432]{1,0:T(8,128)(2,1)} all-gather(bf16[144,432]{1,0:T(8,128)(2,1)S(1)} %copy-done.39), channel_id=1, replica_groups=mesh['ctx'=8,'fsdp'=16] {'ctx'}, dimensions={0}, use_global_device_ids=true | all-gather | bytes 1119744 | tf_op jit(solution)/shard_map/all_gather | solution.py:113
  545.3 33.1 %all_gather.68 = bf16[1152,432]{1,0:T(8,128)(2,1)} all-gather(bf16[144,432]{1,0:T(8,128)(2,1)S(1)} %copy-done.40), channel_id=1, replica_groups=mesh['ctx'=8,'fsdp'=16] {'ctx'}, dimensions={0}, use_global_device_ids=true | all-gather | bytes 1119744 | tf_op jit(solution)/shard_map/all_gather | solution.py:114
  578.5 32.1 %all_gather.69 = bf16[432,1152]{0,1:T(8,128)(2,1)} all-gather(bf16[432,144]{0,1:T(8,128)(2,1)S(1)} %copy-done.41), channel_id=1, replica_groups=mesh['ctx'=8,'fsdp'=16] {'ctx'}, dimensions={1}, use_global_device_ids=true | all-gather | bytes 1119744 | tf_op jit(solution)/shard_map/all_gather | solution.py:115
  622.6 5.4 fusion.89
  628.1 103.4 %reduce-scatter.8.cloned.1.call-done = f32[128,1152]{1,0:T(8,128)} async-done(((f32[2048,1152]{1,0:T(8,128)}), f32[128,1152]{1,0:T(8,128)}) %reduce-scatter.8.cloned.1.call-update) | async-done | bytes 589840 | tf_op jit(solution)/shard_map/reduce_scatter | solution.py:170
  736.7 56.3 %all-gather.12.cloned.1.call-done = bf16[2048,1152]{1,0:T(8,128)(2,1)} async-done(((bf16[128,1152]{1,0:T(8,128)(2,1)}), bf16[2048,1152]{1,0:T(8,128)(2,1)}) %all-gather.12.cloned.1.call-update) | async-done | bytes 4718608 | tf_op jit(solution)/shard_map/all_gather | solution.py:176
  793.0 9.8 multiply_convert_fusion
  805.9 5.4 convolution_add_fusion
  811.6 105.9 %reduce-scatter.10.cloned.1.call-done = f32[128,1152]{1,0:T(8,128)} async-done(((f32[2048,1152]{1,0:T(8,128)}), f32[128,1152]{1,0:T(8,128)}) %reduce-scatter.10.cloned.1.call-update) | async-done | bytes 589840 | tf_op jit(solution)/shard_map/reduce_scatter | solution.py:185
  938.0 25.6 %reduce-scatter.12.cloned.1.call-done = f32[128,256]{1,0:T(8,128)} async-done(((f32[1024,256]{1,0:T(8,128)}), f32[128,256]{1,0:T(8,128)}) %reduce-scatter.12.cloned.1.call-update) | async-done | bytes 131088 | tf_op jit(solution)/shard_map/reduce_scatter | solution.py:224
  967.1 36.8 %reduce-scatter.14.cloned.1.call-done = f32[128,256]{1,0:T(8,128)} async-done(((f32[1024,256]{1,0:T(8,128)}), f32[128,256]{1,0:T(8,128)}) %reduce-scatter.14.cloned.1.call-update) | async-done | bytes 131088 | tf_op jit(solution)/shard_map/reduce_scatter | solution.py:225
  1007.8 6.4 fusion.95
  1015.6 7.5 fusion.93
  1024.7 6.6 fusion.94
  1034.9 65.0 %all-reduce.20 = (f32[1152]{0:T(1024)S(1)}, f32[256]{0:T(256)S(1)}, f32[256]{0:T(256)S(1)}, f32[1152]{0:T(1024)S(1)}, f32[1152]{0:T(1024)S(1)}, /*index=5*/f32[1152]{0:T(1024)S(1)}) all-reduce(f32[1152]{0:T(1024)S(1)} %get-tuple-element.23, f32[256]{0:T(256)S(1)} %copy-done.56, ...), channel_id=6, replica_groups=mesh['ctx'=8,'fsdp'=16] {'ctx','fsdp'}, use_global_device_ids=true, to_apply=%region_20.21.clone | all-reduce | flops 5120 | bytes 40960
  1104.4 72.1 %all-reduce.25.cloned.1.call-done = (f32[1152,1024]{1,0:T(8,128)}, f32[1152,256]{1,0:T(8,128)}, f32[1152,256]{1,0:T(8,128)}, f32[1024,1152]{1,0:T(8,128)}) async-done(((f32[1152,1024]{1,0:T(8,128)}, f32[1152,256]{1,0:T(8,128)}, f32[1152,256]{1,0:T(8,128)}, f32[1024,1152]{1,0:T(8,128)}), (f32[1152,1024]{1,0:T(8,128)}, f32[1152,256]{1,0:T(8,128)}, f32[1152,256]{1,0:T(8,128)}, ...) | async-done | bytes 11796496
  1180.8 40.4 %reduce-scatter.20.cloned.1.call-done = f32[432,144]{0,1:T(8,128)} async-done(((f32[432,1152]{0,1:T(8,128)}), f32[432,144]{0,1:T(8,128)}) %reduce-scatter.20.cloned.1.call-update) | async-done | bytes 248848 | tf_op jit(solution)/shard_map/reduce_scatter | solution.py:189
  1221.1 45.6 %reduce-scatter.16.cloned.1.call-done = f32[144,432]{1,0:T(8,128)} async-done(((f32[1152,432]{1,0:T(8,128)}), f32[144,432]{1,0:T(8,128)}) %reduce-scatter.16.cloned.1.call-update) | async-done | bytes 248848 | tf_op jit(solution)/shard_map/reduce_scatter | solution.py:187
  1266.7 45.5 %reduce-scatter.18.cloned.1.call-done = f32[144,432]{1,0:T(8,128)} async-done(((f32[1152,432]{1,0:T(8,128)}), f32[144,432]{1,0:T(8,128)}) %reduce-scatter.18.cloned.1.call-update) | async-done | bytes 248848 | tf_op jit(solution)/shard_map/reduce_scatter | solution.py:188
  (271 shorter events, 89.7 us)
Async XLA Ops:
  7.2 252.2 %copy-start.47 = (bf16[9,256]{1,0:T(8,128)(2,1)S(1)}, bf16[9,256]{1,0:T(8,128)(2,1)}, u32[]{:S(2)}) copy-start(bf16[9,256]{1,0:T(8,128)(2,1)} %param.26) | copy-start | bytes 13828
  7.2 488.8 %all-gather.14.cloned.1.call-start = ((), (), s32[]{:S(2)}) async-start(), calls=%async_computation.17 | async-start | bytes 4227072 | tf_op jit(solution)/shard_map/all_gather | solution.py:97
  7.9 499.9 %all-gather.8.cloned.1.call-start = ((), (), s32[]{:S(2)}) async-start(), calls=%async_computation.7 | async-start | bytes 2377728 | tf_op jit(solution)/shard_map/all_gather | solution.py:100
  8.7 601.9 %all-gather.10.cloned.1.call-start = ((), (), s32[]{:S(2)}) async-start(), calls=%async_computation.8 | async-start | bytes 5013504 | tf_op jit(solution)/shard_map/all_gather | solution.py:167
  8.7 425.7 %copy-start.57 = (f32[128]{0:T(128)}, f32[128]{0:T(128)S(1)}, u32[]{:S(2)}) copy-start(f32[128]{0:T(128)S(1)} %multiply_power_fusion) | copy-start | bytes 1540
  83.2 351.1 %copy-start.43 = (f32[256]{0:T(256)}, f32[256]{0:T(256)S(1)}, u32[]{:S(2)}) copy-start(f32[256]{0:T(256)S(1)} %convert_element_type.108) | copy-start | bytes 3076
  83.2 422.7 %copy-start.45 = (f32[256]{0:T(256)}, f32[256]{0:T(256)S(1)}, u32[]{:S(2)}) copy-start(f32[256]{0:T(256)S(1)} %convert_element_type.113) | copy-start | bytes 3076
  259.1 174.3 %copy-start.63 = (s32[1,8]{1,0:T(1,128)S(1)}, s32[1,8]{1,0:T(1,128)}, u32[]{:S(2)}) copy-start(s32[1,8]{1,0:T(1,128)} %param.17) | copy-start | bytes 100
  259.1 174.5 %copy-start.2 = (bf16[1,128,1152]{2,1,0:T(8,128)(2,1)S(1)}, bf16[1,128,1152]{2,1,0:T(8,128)(2,1)}, u32[]{:S(2)}) copy-start(bf16[1,128,1152]{2,1,0:T(8,128)(2,1)} %param.16) | copy-start | bytes 884740
  259.3 175.5 %copy-start.17 = (bf16[1152,256]{1,0:T(8,128)(2,1)}, bf16[1152,256]{1,0:T(8,128)(2,1)S(1)}, u32[]{:S(2)}) copy-start(bf16[1152,256]{1,0:T(8,128)(2,1)S(1)} %reshape.359) | copy-start | bytes 1769476
  511.3 406.1 %copy-start.52 = (f32[128]{0:T(128)}, f32[128]{0:T(128)S(1)}, u32[]{:S(2)}) copy-start(f32[128]{0:T(128)S(1)} %fusion.75) | copy-start | bytes 1540
  512.2 219.3 %reduce-scatter.8.cloned.1.call-start = ((), (), s32[]{:S(2)}) async-start(), calls=%async_computation.9 | async-start | bytes 10027008 | tf_op jit(solution)/shard_map/reduce_scatter | solution.py:170
  628.0 104.7 %copy-start.16 = (bf16[1,128,1152]{2,1,0:T(8,128)(2,1)S(1)}, bf16[1,128,1152]{2,1,0:T(8,128)(2,1)}, u32[]{:S(2)}) copy-start(bf16[1,128,1152]{2,1,0:T(8,128)(2,1)} %param.31) | copy-start | bytes 884740
  628.1 164.9 %all-gather.12.cloned.1.call-start = ((), (), s32[]{:S(2)}) async-start(), calls=%async_computation.10 | async-start | bytes 5013504 | tf_op jit(solution)/shard_map/all_gather | solution.py:176
  736.2 181.2 %reduce-scatter.10.cloned.1.call-start = ((), (), s32[]{:S(2)}) async-start(), calls=%async_computation.11 | async-start | bytes 10027008 | tf_op jit(solution)/shard_map/reduce_scatter | solution.py:185
  811.3 107.4 %copy-start.60 = (f32[128]{0:T(128)S(1)}, f32[128]{0:T(128)}, u32[]{:S(2)}) copy-start(f32[128]{0:T(128)} %copy-done.59) | copy-start | bytes 1540
  811.3 107.4 %copy-start.49 = (f32[128]{0:T(128)S(1)}, f32[128]{0:T(128)}, u32[]{:S(2)}) copy-start(f32[128]{0:T(128)} %copy-done.48) | copy-start | bytes 1540
  811.4 109.3 %copy-start.65 = (f32[128]{0:T(128)S(1)}, f32[128]{0:T(128)}, u32[]{:S(2)}) copy-start(f32[128]{0:T(128)} %copy-done.64) | copy-start | bytes 1540
  811.4 152.2 %reduce-scatter.12.cloned.1.call-start = ((), (), s32[]{:S(2)}) async-start(), calls=%async_computation.12 | async-start | bytes 1179648 | tf_op jit(solution)/shard_map/reduce_scatter | solution.py:224
  925.7 78.3 %reduce-scatter.14.cloned.1.call-start = ((), (), s32[]{:S(2)}) async-start(), calls=%async_computation.13 | async-start | bytes 1179648 | tf_op jit(solution)/shard_map/reduce_scatter | solution.py:225
  930.8 245.7 %all-reduce.25.cloned.1.call-start = ((), (), s32[]{:S(2)}) async-start(), calls=%async_computation.18 | async-start | bytes 23592960
  1006.3 214.8 %reduce-scatter.20.cloned.1.call-start = ((), (), s32[]{:S(2)}) async-start(), calls=%async_computation.16 | async-start | bytes 2654208 | tf_op jit(solution)/shard_map/reduce_scatter | solution.py:189
  1014.2 252.5 %reduce-scatter.16.cloned.1.call-start = ((), (), s32[]{:S(2)}) async-start(), calls=%async_computation.14 | async-start | bytes 2654208 | tf_op jit(solution)/shard_map/reduce_scatter | solution.py:187
  1023.1 289.0 %reduce-scatter.18.cloned.1.call-start = ((), (), s32[]{:S(2)}) async-start(), calls=%async_computation.15 | async-start | bytes 2654208 | tf_op jit(solution)/shard_map/reduce_scatter | solution.py:188
  (62 other events, 1101.2 us)
Sparse Core Ops, SparseCore 0:
  9.7 200.7 all-gather.13
  212.2 194.4 all-gather.7
  512.3 62.4 all-gather.9
  628.2 103.2 reduce-scatter.7
  736.4 56.5 all-gather.11
  811.5 105.9 reduce-scatter.9
  925.8 37.7 reduce-scatter.11
  966.0 37.9 reduce-scatter.13
  1009.5 166.8 all-reduce.24
  1179.3 41.7 reduce-scatter.19
  1224.1 42.5 reduce-scatter.15
  1269.5 42.5 reduce-scatter.17
where the time goes:
time: 1330 us; the launch traced here: 1320 us
  blocking collectives  641 us (48%)
  waiting for transfers between devices  533 us (40%)
  matrix products  79.9 us (6%)
  local copies, waits for them, and re-layouts  30.7 us (2%)
  other arithmetic  17.3 us (1%)
  between operations  15.5 us (1%)
    all_gather x1, blocking collectives, body(): lax.all_gather(key_weight, ('ctx', 'fsdp'), axis=0, tiled=True)  176 us
    all_gather x1, blocking collectives, body(): lax.all_gather(value_weight, ('ctx', 'fsdp'), axis=0, tiled=True)  174 us
    unnamed x2, blocking collectives  134 us
    reduce_scatter x1, waiting for transfers between devices, body(): lax.psum_scatter(grad_tokens_all, 'fsdp', scatter_dimension=0, tiled=True)  106 us
    reduce_scatter x1, waiting for transfers between devices, body(): lax.psum_scatter(partial_out, 'fsdp', scatter_dimension=0, tiled=True)  103 us
    unnamed x13, waiting for transfers between devices  73.6 us
    all_gather x1, waiting for transfers between devices, body(): branch_all = lax.all_gather(branch_low, 'fsdp', axis=0, tiled=True)  56.3 us
    reduce_scatter x1, waiting for transfers between devices, body(): lax.psum_scatter(grad_gate, 'ctx', scatter_dimension=0, tiled=True)  45.6 us
  transfers between devices with their start and end apart: 12, of which 9 were waited for; matrix products, arithmetic and copies ran while one was open for 5% of the time, Pallas kernels for 0%

commit v1 on v0

v1 whole, which is shorter than its diff:
```python
from functools import partial

import jax
import jax.numpy as jnp
from jax import lax
from jax.experimental import pallas as pl
from jax.experimental.pallas import tpu as pltpu
from jax.sharding import PartitionSpec as P

EPS = 1e-06
SCALE = 0.0625
BASE = 1000000.0
MASKED = -1e30
BF16 = jnp.bfloat16
F32 = jnp.float32
VMEM_BYTES = 56 * 1024 * 1024


def rms_norm(values, gain):
    return values * lax.rsqrt(jnp.mean(values * values, axis=-1, keepdims=True) + EPS) * gain


def rotary(values, cosines, sines):
    half = values.shape[-1] // 2
    first = values[..., :half]
    second = values[..., half:]
    return jnp.concatenate(
        [first * cosines - second * sines, second * cosines + first * sines], axis=-1
    )


def angles(positions, width):
    half = width // 2
    freqs = BASE ** (-jnp.arange(half, dtype=jnp.float32) / half)
    return positions.astype(jnp.float32)[:, None] * freqs[None, :]


def token_positions(pairs, tok_rows):
    half = tok_rows // 2
    index = jnp.arange(tok_rows, dtype=jnp.int32)
    count = 2 * pairs.shape[0]
    blocks = jnp.where(index[None, :] < half, pairs[:, None], count - 1 - pairs[:, None])
    return blocks * half + index[None, :] % half


def matmul(left, right):
    return jnp.dot(left, right, preferred_element_type=jnp.float32)


def matmul_tn(left, right):
    return lax.dot_general(
        left, right, (((0,), (0,)), ((), ())), preferred_element_type=jnp.float32
    )


def matmul_nt(left, right):
    return lax.dot_general(
        left, right, (((1,), (1,)), ((), ())), preferred_element_type=jnp.float32
    )


def score_block(query_low, key_all, causal):
    scores = (
        jnp.einsum("thd,kd->htk", query_low, key_all, preferred_element_type=jnp.float32) * SCALE
    )
    return jnp.where(causal[None], scores, MASKED)


def here():
    ctx = lax.axis_index("ctx")
    fsdp = lax.axis_index("fsdp")
    return {
        "x": lax.rem(ctx, 4),
        "y": lax.div(fsdp, 4),
        "z": lax.rem(lax.div(fsdp, 2), 2) * 2 + lax.div(ctx, 4),
        "core": lax.rem(fsdp, 2),
    }


class Net:
    def __init__(self, send_sems, recv_sems):
        self.me = here()
        self.send_sems, self.recv_sems = send_sems, recv_sems
        self.used = 0
        self.sent = []

    def device(self, **moved):
        at = {**self.me, **moved}
        return (
            lax.rem(at["z"], 2) * 4 + at["x"],
            at["y"] * 4 + lax.div(at["z"], 2) * 2 + at["core"],
        )

    def step(self, axis, by):
        return lax.rem(self.me[axis] + by, 4)

    def neighbour(self, axis, by):
        return self.device(**{axis: self.step(axis, by)})

    def sibling(self):
        return self.device(core=1 - self.me["core"])

    def mirror(self):
        z = self.me["z"]
        return self.device(z=z + 1 - 2 * lax.rem(z, 2))

    def barrier(self, peers):
        sem = pltpu.get_barrier_semaphore()
        for peer in peers:
            pl.semaphore_signal(sem, inc=1, device_id=peer, device_id_type=pl.DeviceIdType.MESH)
        pl.semaphore_wait(sem, len(peers))

    def send(self, src, dst, peer):
        n = self.used
        self.used += 1
        copy = pltpu.make_async_remote_copy(
            src_ref=src,
            dst_ref=dst,
            send_sem=self.send_sems.at[n],
            recv_sem=self.recv_sems.at[n],
            device_id=peer,
            device_id_type=pl.DeviceIdType.MESH,
        )
        copy.start()
        self.sent.append(copy)
        return copy

    def send_done(self):
        for copy in self.sent:
            copy.wait_send()


def interleave(*tasks):
    tasks = list(tasks)
    while tasks:
        for task in list(tasks):
            try:
                next(task)
            except StopIteration:
                tasks.remove(task)


def gather_ring(net, axis, own, place, arrived=None):
    mine = net.me[axis]
    left, right, far = net.step(axis, 3), net.step(axis, 1), net.step(axis, 2)
    to_left, to_right = net.neighbour(axis, 3), net.neighbour(axis, 1)
    r0 = net.send(own(0), place(mine, 0), to_right)
    l1 = net.send(own(1), place(mine, 1), to_left)
    r1 = net.send(own(1), place(mine, 1), to_right)
    l0 = net.send(own(0), place(mine, 0), to_left)
    yield
    r0.wait_recv()
    f0 = net.send(place(left, 0), place(left, 0), to_right)
    yield
    l1.wait_recv()
    f1 = net.send(place(right, 1), place(right, 1), to_left)
    yield
    r1.wait_recv()
    if arrived:
        arrived(left)
    yield
    l0.wait_recv()
    if arrived:
        arrived(right)
    yield
    f0.wait_recv()
    f1.wait_recv()
    if arrived:
        arrived(far)


def scatter_ring(net, axis, part, bufs, total):
    mine = net.me[axis]
    left, right, far = net.step(axis, 3), net.step(axis, 1), net.step(axis, 2)
    to_left, to_right = net.neighbour(axis, 3), net.neighbour(axis, 1)
    from_left, from_right, hold, stage = bufs
    a0 = net.send(part(far, 0), hold.at[0], to_right)
    a1 = net.send(part(far, 1), hold.at[1], to_left)
    r1 = net.send(part(right, 1), from_left.at[1], to_right)
    l0 = net.send(part(left, 0), from_right.at[0], to_left)
    yield
    a0.wait_recv()
    stage[0] = (part(right, 0)[...].astype(F32) + hold[0].astype(F32)).astype(BF16)
    r0 = net.send(stage.at[0], from_left.at[0], to_right)
    yield
    a1.wait_recv()
    stage[1] = (part(left, 1)[...].astype(F32) + hold[1].astype(F32)).astype(BF16)
    l1 = net.send(stage.at[1], from_right.at[1], to_left)
    yield
    l0.wait_recv()
    r0.wait_recv()
    total(0, (part(mine, 0), from_left.at[0], from_right.at[0]))
    yield
    r1.wait_recv()
    l1.wait_recv()
    total(1, (part(mine, 1), from_left.at[1], from_right.at[1]))


def add_up(terms):
    out = terms[0][...].astype(F32)
    for term in terms[1:]:
        out = out + term[...].astype(F32)
    return out


def sems(count):
    return [pltpu.SemaphoreType.DMA((count,)), pltpu.SemaphoreType.DMA((count,))]


def call(kernel, name, out_shape, in_spaces, out_spaces, scratch, number):
    return pl.pallas_call(
        kernel,
        name=name,
        out_shape=out_shape,
        in_specs=[pl.BlockSpec(memory_space=space) for space in in_spaces],
        out_specs=[pl.BlockSpec(memory_space=space) for space in out_spaces],
        scratch_shapes=scratch,
        compiler_params=pltpu.CompilerParams(
            collective_id=number, has_side_effects=True, vmem_limit_bytes=VMEM_BYTES
        ),
    )


ORDERS = ("xyz", "yzx", "zxy")
BLOB = 192
PART = BLOB // 3
HALF = PART // 2
FFN_ROWS = (((0, 48), (48, 32)), ((80, 32), (112, 32)))


def grid_at(ref, have, sel, tail):
    index = []
    every = slice(None)
    if "z" in have:
        index.append(lax.rem(sel["z"], 2) if "z" in sel else every)
    for axis in "xy":
        if axis in have:
            index.append(sel.get(axis, every))
    if "z" in have:
        index.append(lax.div(sel["z"], 2) if "z" in sel else every)
    return ref.at[tuple(index) + tail]


def weights_kernel(blob, ffn, all_blobs, all_ffn, send_sems, recv_sems, local_sems):
    net = Net(send_sems, recv_sems)
    me = net.me
    sibling = net.sibling()
    net.barrier([net.neighbour(axis, by) for axis in "xyz" for by in (1, 3)] + [sibling])
    core = me["core"]
    own_blob = pltpu.make_async_copy(
        blob, grid_at(all_blobs, "xyz", me, (core,)), local_sems.at[0]
    )
    own_blob.start()
    own_ffn = pltpu.make_async_copy(ffn, all_ffn.at[:, me["z"], me["x"]], local_sems.at[1])
    own_ffn.start()
    forwards = []

    def blob_task(order, start):
        def rows(h):
            return pl.ds(start + h * HALF, HALF)

        both = pl.ds(start, PART)
        known = dict(me)
        for count, axis in enumerate(order):
            fixed = {k: me[k] for k in order[count + 1 :]}

            def place(k, h):
                return grid_at(all_blobs, "xyz", {**fixed, axis: k}, (core, rows(h)))

            def own(h):
                if count == 0:
                    return blob.at[rows(h)]
                return place(me[axis], h)

            def forward(k):
                ref = grid_at(all_blobs, "xyz", {**fixed, axis: k}, (core, both))
                forwards.append(net.send(ref, ref, sibling))

            if count == 2:
                forward(me[axis])
            yield from gather_ring(net, axis, own, place, forward if count == 2 else None)
            if count == 0 and start == 0:
                own_blob.wait()
            yield

    def ffn_task(order, rows):
        first, second = order
        fixed = me[second]

        def spot(i, j, h):
            ix, iz = (i, j) if first == "x" else (j, i)
            return all_ffn.at[:, iz, ix, pl.ds(*rows[h])]

        yield from gather_ring(
            net, first, lambda h: ffn.at[:, pl.ds(*rows[h])], lambda k, h: spot(k, fixed, h)
        )
        if first == "x":
            own_ffn.wait()
        yield
        yield from gather_ring(
            net,
            second,
            lambda h: spot(slice(None), fixed, h),
            lambda k, h: spot(slice(None), k, h),
        )

    interleave(*(blob_task(order, i * PART) for i, order in enumerate(ORDERS)))
    interleave(ffn_task("xz", FFN_ROWS[0]), ffn_task("zx", FFN_ROWS[1]))
    for copy in forwards:
        copy.wait_recv()
    net.send_done()


def gather_weights(blob, ffn):
    any_ = pl.ANY
    return call(
        weights_kernel,
        "gather_weights",
        [
            jax.ShapeDtypeStruct((2, 4, 4, 2, 2, BLOB, 128), BF16),
            jax.ShapeDtypeStruct((3, 4, 4) + ffn.shape[1:], BF16),
        ],
        [any_, any_],
        [any_, any_],
        sems(3 * (18 + 4) + 24) + [pltpu.SemaphoreType.DMA((2,))],
        1,
    )(blob, ffn)


def grads_kernel(blob, ffn, blob_out, ffn_out, send_sems, recv_sems, *bufs):
    net = Net(send_sems, recv_sems)
    me = net.me
    bufs = list(bufs)
    sibling = net.sibling()
    net.barrier([net.neighbour(axis, by) for axis in "xyz" for by in (1, 3)] + [sibling])
    core = me["core"]
    every = slice(None)
    paired = bufs.pop(0)
    copies = []
    for i in range(3):
        rows = pl.ds(i * PART, PART)
        copies.append(
            net.send(
                blob.at[every, every, every, every, 1 - core, rows],
                paired.at[every, every, every, every, rows],
                sibling,
            )
        )

    def blob_task(order, start, copy, own_bufs):
        own_bufs = list(own_bufs)
        yield
        copy.wait_recv()
        rows = pl.ds(start, PART)
        for a in range(2):
            for b in range(4):
                paired[a, b, :, :, rows] = (
                    paired[a, b, :, :, rows].astype(F32) + blob[a, b, :, :, core, rows].astype(F32)
                ).astype(BF16)
        source, offset = paired, start
        for count, axis in enumerate(order):
            have = order[count:]
            result = own_bufs[4] if count < 2 else None

            def part(k, h, source=source, offset=offset, have=have, axis=axis):
                return grid_at(source, have, {axis: k}, (pl.ds(offset + h * HALF, HALF),))

            def total(h, terms, result=result, count=count, have=have):
                if count < 2:
                    grid_at(result, have[1:], {}, (pl.ds(h * HALF, HALF),))[...] = add_up(
                        terms
                    ).astype(BF16)
                else:
                    blob_out[pl.ds(start + h * HALF, HALF)] = add_up(terms)

            yield from scatter_ring(net, axis, part, own_bufs[:4], total)
            yield
            source, offset = result, 0
            own_bufs = own_bufs[5:]

    def ffn_task(order, rows, own_bufs):
        first, second = order
        fl, fr, hold, stage, result, fl2, fr2, hold2, stage2 = own_bufs

        def cut(bufs, h):
            return tuple(buf.at[:, :, :, pl.ds(0, rows[h][1])] for buf in bufs)

        low = rows[0][0]

        def part(k, h):
            if first == "x":
                return ffn.at[:, :, k, pl.ds(*rows[h])]
            return ffn.at[:, k, :, pl.ds(*rows[h])]

        def total(h, terms):
            result[:, :, pl.ds(rows[h][0] - low, rows[h][1])] = add_up(terms).astype(BF16)

        def part2(k, h):
            return result.at[:, k, pl.ds(rows[h][0] - low, rows[h][1])]

        def total2(h, terms):
            ffn_out[:, pl.ds(*rows[h])] = add_up(terms)

        yield from scatter_uneven(net, first, part, (fl, fr, hold, stage), rows, total)
        yield
        yield from scatter_uneven(net, second, part2, (fl2, fr2, hold2, stage2), rows, total2)

    tasks = []
    for i, order in enumerate(ORDERS):
        tasks.append(blob_task(order, i * PART, copies[i], bufs[:14]))
        bufs = bufs[14:]
    interleave(
        ffn_task("xz", FFN_ROWS[0], bufs[:9]), ffn_task("zx", FFN_ROWS[1], bufs[9:]), *tasks
    )
    net.send_done()


class Cut:
    def __init__(self, ref, rows):
        self.ref, self.rows = ref, rows

    @property
    def at(self):
        return self

    def __getitem__(self, h):
        ref = self.ref.at[h]
        lead = (slice(None),) * (len(ref.shape) - 2)
        return ref.at[lead + (pl.ds(0, self.rows[h][1]),)]


def scatter_uneven(net, axis, part, bufs, rows, total):
    mine = net.me[axis]
    left, right, far = net.step(axis, 3), net.step(axis, 1), net.step(axis, 2)
    to_left, to_right = net.neighbour(axis, 3), net.neighbour(axis, 1)
    from_left, from_right, hold, stage = (Cut(buf, rows) for buf in bufs)
    a0 = net.send(part(far, 0), hold[0], to_right)
    a1 = net.send(part(far, 1), hold[1], to_left)
    r1 = net.send(part(right, 1), from_left[1], to_right)
    l0 = net.send(part(left, 0), from_right[0], to_left)
    yield
    a0.wait_recv()
    stage[0][...] = (part(right, 0)[...].astype(F32) + hold[0][...].astype(F32)).astype(BF16)
    r0 = net.send(stage[0], from_left[0], to_right)
    yield
    a1.wait_recv()
    stage[1][...] = (part(left, 1)[...].astype(F32) + hold[1][...].astype(F32)).astype(BF16)
    l1 = net.send(stage[1], from_right[1], to_left)
    yield
    l0.wait_recv()
    r0.wait_recv()
    total(0, (part(mine, 0), from_left[0], from_right[0]))
    yield
    r1.wait_recv()
    l1.wait_recv()
    total(1, (part(mine, 1), from_left[1], from_right[1]))


def lead_dims(have):
    dims = []
    if "z" in have:
        dims.append(2)
    dims += [4 for axis in "xy" if axis in have]
    if "z" in have:
        dims.append(2)
    return tuple(dims)


def scatter_grads(blob, ffn):
    wide = ffn.shape[-1]
    scratch = sems(3 * 19 + 24) + [pltpu.VMEM((2, 4, 4, 2, BLOB, 128), BF16)]
    for order in ORDERS:
        for count in range(3):
            left = lead_dims(order[count + 1 :])
            scratch += [pltpu.VMEM((2,) + left + (HALF, 128), BF16)] * 4
            if count < 2:
                scratch.append(pltpu.VMEM(left + (PART, 128), BF16))
    for rows in FFN_ROWS:
        most = max(rows[0][1], rows[1][1])
        every = rows[0][1] + rows[1][1]
        scratch += [pltpu.VMEM((2, 3, 4, most, wide), BF16)] * 4
        scratch.append(pltpu.VMEM((3, 4, every, wide), BF16))
        scratch += [pltpu.VMEM((2, 3, most, wide), BF16)] * 4
    vmem = pltpu.VMEM
    return call(
        grads_kernel,
        "scatter_grads",
        [
            jax.ShapeDtypeStruct((BLOB, 128), F32),
            jax.ShapeDtypeStruct((3,) + ffn.shape[3:], F32),
        ],
        [vmem, vmem],
        [vmem, vmem],
        scratch,
        2,
    )(blob, ffn)


def keys_kernel(key, value, keys, values, send_sems, recv_sems, local_sems):
    net = Net(send_sems, recv_sems)
    me = net.me
    mirror = net.mirror()
    net.barrier([net.neighbour("x", 1), net.neighbour("x", 3), mirror])
    low, x = lax.rem(me["z"], 2), me["x"]
    own_key = pltpu.make_async_copy(key, keys.at[low, x], local_sems.at[0])
    own_value = pltpu.make_async_copy(value, values.at[low, x], local_sems.at[1])
    own_key.start()
    own_value.start()
    half = key.shape[0] // 2

    def rows(h):
        return pl.ds(h * half, half)

    def key_task():
        swap = net.send(key, keys.at[low, x], mirror)
        yield
        own_key.wait()
        swap.wait_recv()
        yield from gather_ring(
            net, "x", lambda h: keys.at[:, x, rows(h)], lambda k, h: keys.at[:, k, rows(h)]
        )

    def value_task():
        yield from gather_ring(
            net, "x", lambda h: value.at[rows(h)], lambda k, h: values.at[low, k, rows(h)]
        )
        own_value.wait()
        swap = net.send(values.at[low], values.at[low], mirror)
        yield
        swap.wait_recv()

    interleave(key_task(), value_task())
    net.send_done()


def gather_keys(key, value):
    any_ = pl.ANY
    return call(
        keys_kernel,
        "gather_keys",
        [jax.ShapeDtypeStruct((2, 4) + key.shape, BF16)] * 2,
        [any_, any_],
        [any_, any_],
        sems(14) + [pltpu.SemaphoreType.DMA((2,))],
        3,
    )(key, value)


def key_grads_kernel(keys, values, key, value, send_sems, recv_sems, *bufs):
    net = Net(send_sems, recv_sems)
    me = net.me
    mirror = net.mirror()
    net.barrier([net.neighbour("x", 1), net.neighbour("x", 3), mirror])
    low = lax.rem(me["z"], 2)
    half = key.shape[0] // 2
    key_bufs, value_bufs = bufs[:4], bufs[4:8]
    key_pair, key_sent, value_pair = bufs[8:]

    def rows(h):
        return pl.ds(h * half, half)

    def key_task():
        def total(h, terms):
            key_sent[:, rows(h)] = add_up(terms).astype(BF16)

        yield from scatter_ring(
            net, "x", lambda k, h: keys.at[:, k, rows(h)], key_bufs, total
        )
        swap = net.send(key_sent.at[1 - low], key_pair, mirror)
        yield
        swap.wait_recv()
        key[...] = add_up((key_sent.at[low], key_pair))

    def value_task():
        swap = net.send(values.at[1 - low], value_pair, mirror)
        yield
        swap.wait_recv()
        value_pair[...] = add_up((value_pair, values.at[low])).astype(BF16)

        def total(h, terms):
            value[rows(h)] = add_up(terms)

        yield from scatter_ring(
            net, "x", lambda k, h: value_pair.at[k, rows(h)], value_bufs, total
        )

    interleave(key_task(), value_task())
    net.send_done()


def scatter_key_grads(keys, values):
    rows, width = keys.shape[2:]
    vmem = pltpu.VMEM
    return call(
        key_grads_kernel,
        "scatter_key_grads",
        [jax.ShapeDtypeStruct((rows, width), F32)] * 2,
        [vmem, vmem],
        [vmem, vmem],
        sems(14)
        + [pltpu.VMEM((2, 2, rows // 2, width), BF16)] * 4
        + [pltpu.VMEM((2, rows // 2, width), BF16)] * 4
        + [
            pltpu.VMEM((rows, width), BF16),
            pltpu.VMEM((2, rows, width), BF16),
            pltpu.VMEM((4, rows, width), BF16),
        ],
        4,
    )(keys, values)


def tokens_kernel(own, out, send_sems, recv_sems, local_sems):
    net = Net(send_sems, recv_sems)
    me = net.me
    sibling = net.sibling()
    net.barrier([net.neighbour("y", 1), net.neighbour("y", 3), sibling])
    core, y = me["core"], me["y"]
    local = pltpu.make_async_copy(own, out.at[y, core], local_sems.at[0])
    local.start()
    half = own.shape[0] // 2
    forwards = [net.send(own, out.at[y, core], sibling)]

    def forward(k):
        forwards.append(net.send(out.at[k, core], out.at[k, core], sibling))

    def rows(h):
        return pl.ds(h * half, half)

    interleave(
        gather_ring(
            net,
            "y",
            lambda h: own.at[rows(h)],
            lambda k, h: out.at[k, core, rows(h)],
            forward,
        )
    )
    for copy in forwards:
        copy.wait_recv()
    local.wait()
    net.send_done()


def gather_tokens(own, number):
    any_ = pl.ANY
    return call(
        tokens_kernel,
        f"gather_tokens_{number}",
        [jax.ShapeDtypeStruct((4, 2) + own.shape, BF16)],
        [any_],
        [any_],
        sems(10) + [pltpu.SemaphoreType.DMA((1,))],
        number,
    )(own)[0]


def sums_kernel(parts, out, send_sems, recv_sems, paired, *bufs):
    net = Net(send_sems, recv_sems)
    me = net.me
    sibling = net.sibling()
    net.barrier([net.neighbour("y", 1), net.neighbour("y", 3), sibling])
    core = me["core"]
    half = out.shape[0] // 2
    order = [net.step("y", by) for by in (2, 1, 3)] + [me["y"]]
    copies = [net.send(parts.at[k, 1 - core], paired.at[k], sibling) for k in order]
    for k, copy in zip(order, copies):
        copy.wait_recv()
        paired[k] = (paired[k].astype(F32) + parts[k, core].astype(F32)).astype(BF16)

    def rows(h):
        return pl.ds(h * half, half)

    def total(h, terms):
        out[rows(h)] = add_up(terms)

    interleave(scatter_ring(net, "y", lambda k, h: paired.at[k, rows(h)], bufs, total))
    net.send_done()


def scatter_sums(parts, number):
    rows, width = parts.shape[2:]
    vmem = pltpu.VMEM
    return call(
        sums_kernel,
        f"scatter_sums_{number}",
        [jax.ShapeDtypeStruct((rows, width), F32)],
        [vmem],
        [vmem],
        sems(10)
        + [pltpu.VMEM((4, rows, width), BF16)]
        + [pltpu.VMEM((2, rows // 2, width), BF16)] * 4,
        number,
    )(parts)[0]


def body(
    inputs,
    pair_order,
    attn_gain,
    query_gain,
    key_gain,
    mixer_gain,
    ffn_gain,
    branch_gain,
    query_weight,
    key_weight,
    value_weight,
    output_weight,
    gate_weight,
    up_weight,
    down_weight,
    cotangent,
):
    gains = (attn_gain, query_gain, key_gain, mixer_gain, ffn_gain, branch_gain)
    n_dev = 128
    width = inputs.shape[2]
    rows = inputs.shape[1]
    head_dim = key_weight.shape[1]
    qw = query_weight.shape[1]
    heads = qw // head_dim
    d_own = query_weight.shape[0]
    o_own = output_weight.shape[0]
    qkv_w = qw + 2 * head_dim
    qkv_rows = d_own * qkv_w // 128
    out_rows = o_own * width // 128
    qkv_pad = 112

    gain_row = jnp.concatenate(gains)
    n_gain = gain_row.shape[0]
    gain_row = jnp.pad(gain_row, (0, (qkv_pad - qkv_rows) * 128 - n_gain))
    blob = jnp.concatenate(
        [
            jnp.concatenate([query_weight, key_weight, value_weight], axis=1).reshape(
                qkv_rows, 128
            ),
            gain_row.reshape(qkv_pad - qkv_rows, 128),
            output_weight.reshape(out_rows, 128),
            jnp.zeros((BLOB - qkv_pad - out_rows, 128), BF16),
        ]
    )
    ffn_own = jnp.stack([gate_weight, up_weight, down_weight.T])
    all_blobs, all_ffn = gather_weights(blob, ffn_own)
    all_blobs = all_blobs.reshape(n_dev, BLOB, 128)
    qkv_all = all_blobs[:, :qkv_rows].reshape(n_dev * d_own, qkv_w)
    output_all_w = all_blobs[:, qkv_pad : qkv_pad + out_rows].reshape(n_dev * o_own, width)
    gain_all = all_blobs[:, qkv_rows, :n_gain].astype(F32)
    full_gains = []
    at = 0
    for gain in gains:
        full_gains.append(gain_all[:, at : at + gain.shape[0]].reshape(-1))
        at += gain.shape[0]
    gain_in, gain_query, gain_key, gain_mixed, gain_ffn, gain_branch = full_gains
    ff_own = gate_weight.shape[1]
    all_ffn = all_ffn.reshape(3, 2, width, ff_own)

    slot = lax.axis_index("ctx")
    all_positions = token_positions(pair_order[0], rows).reshape(-1)
    own_positions = lax.dynamic_slice_in_dim(all_positions, slot * rows, rows)
    angle = angles(own_positions, head_dim)
    cosines = jnp.cos(angle)
    sines = jnp.sin(angle)
    causal = all_positions[None, :] <= own_positions[:, None]
    hidden_in = inputs[0].astype(jnp.float32)
    normed_in, norm_in_back = jax.vjp(rms_norm, hidden_in, gain_in)
    attn_input = normed_in.astype(jnp.bfloat16)
    qkv_raw = matmul(attn_input, qkv_all)
    queries_raw = qkv_raw[:, :qw]
    keys_raw = qkv_raw[:, qw : qw + head_dim]
    values_raw = qkv_raw[:, qw + head_dim :]

    def query_shape(raw, gain):
        return rotary(
            rms_norm(raw.reshape(rows, heads, head_dim), gain),
            cosines[:, None, :],
            sines[:, None, :],
        )

    def key_shape(raw, gain):
        return rotary(rms_norm(raw, gain), cosines, sines)

    queries_rot, query_back = jax.vjp(query_shape, queries_raw, gain_query)
    keys_rot, key_back = jax.vjp(key_shape, keys_raw, gain_key)
    query_low = queries_rot.astype(jnp.bfloat16)
    key_low = keys_rot.astype(jnp.bfloat16)
    value_low = values_raw.astype(jnp.bfloat16)
    key_all, value_all = gather_keys(key_low, value_low)
    key_all = key_all.reshape(-1, head_dim)
    value_all = value_all.reshape(-1, head_dim)
    scores = score_block(query_low, key_all, causal)
    peak = jnp.max(scores, axis=-1, keepdims=True)
    expo = jnp.exp(scores - peak)
    total = jnp.sum(expo, axis=-1, keepdims=True)
    probs = expo / total
    probs_low = probs.astype(jnp.bfloat16)
    mixed = jnp.einsum("htk,kd->thd", probs_low, value_all, preferred_element_type=jnp.float32)
    mixed_low = mixed.reshape(rows, heads * head_dim).astype(jnp.bfloat16)
    attn_out = matmul(mixed_low, output_all_w)
    post_attn, post_attn_back = jax.vjp(rms_norm, attn_out, gain_mixed)
    resid = hidden_in + post_attn
    normed_mid, mid_back = jax.vjp(rms_norm, resid, gain_ffn)
    ffn_input = normed_mid.astype(jnp.bfloat16)
    tokens_all = gather_tokens(ffn_input, 5).reshape(-1, width)

    fronts = []
    partial_out = 0.0
    for j in range(2):
        gate_pre = matmul(tokens_all, all_ffn[0, j])
        up_pre = matmul(tokens_all, all_ffn[1, j])
        activated, gelu_back = jax.vjp(partial(jax.nn.gelu, approximate=True), gate_pre)
        hidden_low = (activated * up_pre).astype(jnp.bfloat16)
        fronts.append((up_pre, activated, gelu_back, hidden_low))
        partial_out = partial_out + matmul_nt(hidden_low, all_ffn[2, j])
    branch_raw = scatter_sums(partial_out.astype(BF16).reshape(4, 2, rows, width), 6)
    post_ffn, post_ffn_back = jax.vjp(rms_norm, branch_raw, gain_branch)
    outputs = (resid + post_ffn)[None]
    upstream = cotangent[0].astype(jnp.float32)
    grad_branch, grad_gain_branch = post_ffn_back(upstream)
    branch_low = grad_branch.astype(jnp.bfloat16)
    branch_all = gather_tokens(branch_low, 7).reshape(-1, width)
    grad_tokens_all = 0.0
    ffn_grads = [[], [], []]
    for j in range(2):
        up_pre, activated, gelu_back, hidden_low = fronts[j]
        grad_hidden = matmul(branch_all, all_ffn[2, j])
        ffn_grads[2].append(matmul_tn(branch_all, hidden_low))
        gate_low = gelu_back(grad_hidden * up_pre)[0].astype(jnp.bfloat16)
        up_low = (grad_hidden * activated).astype(jnp.bfloat16)
        grad_tokens_all = (
            grad_tokens_all
            + matmul_nt(gate_low, all_ffn[0, j])
            + matmul_nt(up_low, all_ffn[1, j])
        )
        ffn_grads[0].append(matmul_tn(tokens_all, gate_low))
        ffn_grads[1].append(matmul_tn(tokens_all, up_low))
    ffn_grads = jnp.stack([jnp.stack([g.astype(BF16) for g in pair]) for pair in ffn_grads])
    ffn_grads = ffn_grads.reshape(3, 4, 4, width // 8, ff_own)
    grad_ffn_input = scatter_sums(grad_tokens_all.astype(BF16).reshape(4, 2, rows, width), 8)
    grad_resid_mid, grad_gain_ffn = mid_back(grad_ffn_input)
    grad_resid = upstream + grad_resid_mid
    grad_attn_out, grad_gain_mixed = post_attn_back(grad_resid)
    attn_low = grad_attn_out.astype(jnp.bfloat16)
    grad_mixed = matmul_nt(attn_low, output_all_w)
    grad_output_w = matmul_tn(mixed_low, attn_low)
    mixed_grad_low = grad_mixed.astype(jnp.bfloat16).reshape(rows, heads, head_dim)
    grad_value_all = jnp.einsum(
        "htk,thd->kd", probs_low, mixed_grad_low, preferred_element_type=jnp.float32
    )
    grad_probs = jnp.einsum(
        "thd,kd->htk", mixed_grad_low, value_all, preferred_element_type=jnp.float32
    )
    delta = jnp.sum(grad_probs * probs, axis=-1, keepdims=True)
    grad_scores_low = (probs * (grad_probs - delta)).astype(jnp.bfloat16)
    grad_query_rot = (
        jnp.einsum("htk,kd->thd", grad_scores_low, key_all, preferred_element_type=jnp.float32)
        * SCALE
    )
    grad_key_all = (
        jnp.einsum("htk,thd->kd", grad_scores_low, query_low, preferred_element_type=jnp.float32)
        * SCALE
    )
    grad_key_rot, grad_value = scatter_key_grads(
        grad_key_all.astype(BF16).reshape(2, 4, rows, head_dim),
        grad_value_all.astype(BF16).reshape(2, 4, rows, head_dim),
    )
    grad_query_raw, grad_gain_query = query_back(grad_query_rot)
    grad_key_raw, grad_gain_key = key_back(grad_key_rot)
    glow = jnp.concatenate([grad_query_raw, grad_key_raw, grad_value], axis=1).astype(BF16)
    grad_attn_input = matmul_nt(glow, qkv_all)
    grad_qkv_w = matmul_tn(attn_input, glow)
    grad_hidden_in, grad_gain_in = norm_in_back(grad_attn_input)
    inputs_grad = (grad_resid + grad_hidden_in)[None]
    gain_grads = (
        grad_gain_in,
        grad_gain_query,
        grad_gain_key,
        grad_gain_mixed,
        grad_gain_ffn,
        grad_gain_branch,
    )
    gain_rows = jnp.concatenate([g.astype(BF16).reshape(n_dev, -1) for g in gain_grads], axis=1)
    gain_rows = jnp.pad(gain_rows, ((0, 0), (0, (qkv_pad - qkv_rows) * 128 - n_gain)))
    grad_blobs = jnp.concatenate(
        [
            grad_qkv_w.astype(BF16).reshape(n_dev, qkv_rows, 128),
            gain_rows.reshape(n_dev, qkv_pad - qkv_rows, 128),
            grad_output_w.astype(BF16).reshape(n_dev, out_rows, 128),
            jnp.zeros((n_dev, BLOB - qkv_pad - out_rows, 128), BF16),
        ],
        axis=1,
    ).reshape(2, 4, 4, 2, 2, BLOB, 128)
    blob_sum, ffn_sum = scatter_grads(grad_blobs, ffn_grads)
    qkv_sum = blob_sum[:qkv_rows].reshape(d_own, qkv_w)
    out_sum = blob_sum[qkv_pad : qkv_pad + out_rows].reshape(o_own, width)
    gain_sums = []
    at = 0
    for gain in gains:
        gain_sums.append(blob_sum[qkv_rows, at : at + gain.shape[0]])
        at += gain.shape[0]
    return (
        outputs,
        inputs_grad,
        *gain_sums,
        qkv_sum[:, :qw],
        qkv_sum[:, qw : qw + head_dim],
        qkv_sum[:, qw + head_dim :],
        out_sum,
        ffn_sum[0],
        ffn_sum[1],
        ffn_sum[2].T,
    )


def solution(mesh):
    placed = (
        P("fsdp", "ctx", None),
        P("fsdp", None),
        P(("ctx", "fsdp")),
        P(("ctx", "fsdp")),
        P(("ctx", "fsdp")),
        P(("ctx", "fsdp")),
        P(("ctx", "fsdp")),
        P(("ctx", "fsdp")),
        P(("ctx", "fsdp"), None),
        P(("ctx", "fsdp"), None),
        P(("ctx", "fsdp"), None),
        P(("ctx", "fsdp"), None),
        P("ctx", "fsdp"),
        P("ctx", "fsdp"),
        P("fsdp", "ctx"),
        P("fsdp", "ctx", None),
    )
    return jax.shard_map(
        body,
        mesh=mesh,
        in_specs=placed,
        out_specs=(
            P("fsdp", "ctx", None),
            P("fsdp", "ctx", None),
            P(("ctx", "fsdp")),
            P(("ctx", "fsdp")),
            P(("ctx", "fsdp")),
            P(("ctx", "fsdp")),
            P(("ctx", "fsdp")),
            P(("ctx", "fsdp")),
            P(("ctx", "fsdp"), None),
            P(("ctx", "fsdp"), None),
            P(("ctx", "fsdp"), None),
            P(("ctx", "fsdp"), None),
            P("ctx", "fsdp"),
            P("ctx", "fsdp"),
            P("fsdp", "ctx"),
        ),
        check_vma=False,
    )
```

time: 1330 us -> 472 us (0.35)
  blocking collectives: 641 us -> 0 us
  waiting for transfers between devices: 533 us -> 0 us
  Pallas kernels: 0 us -> 259 us
  local copies, waits for them, and re-layouts: 30.7 us -> 80.8 us
  other arithmetic: 17.3 us -> 51.4 us
  between operations: 15.5 us -> 2.11 us
    all_gather x7 -> x0, blocking collectives: 508 us -> none  [the longest x1 176 us: body(): lax.all_gather(key_weight, ('ctx', 'fsdp'), axis=0, tiled=True)]
    reduce_scatter x7 -> x0, waiting for transfers between devices: 403 us -> none  [the longest x1 106 us: body(): lax.psum_scatter(grad_tokens_all, 'fsdp', scatter_dimension=0, tiled=True)]
    pallas_call x0 -> x8, Pallas kernels: none -> 259 us  [the longest x1 77.3 us: scatter_grads(): call(grads_kernel, 'scatter_grads', [jax.ShapeDtypeStruct((BLOB, 128), F3...]
    unnamed x2 -> x0, blocking collectives: 134 us -> none
    unnamed x13 -> x0, waiting for transfers between devices: 73.6 us -> none
    all_gather x4 -> x0, waiting for transfers between devices: 56.3 us -> none  [the longest x1 56.3 us: body(): branch_all = lax.all_gather(branch_low, 'fsdp', axis=0, tiled=True)]
    unnamed x172 -> x177, local copies, waits for them, and re-layouts: 27.6 us -> 4.3 us
    another operation x1 -> x9, other arithmetic: 0.08 us -> 18.4 us  [the longest x1 6.78 us: body(): jnp.stack([jnp.stack([g.astype(BF16) for g in pair]) for pair in ffn_grads])]
  transfers between devices with their start and end apart: 12 -> 0, of which waited for: 9 -> 0; matrix products, arithmetic and copies ran while one was open for 5% -> 0% of each run, Pallas kernels for 0% -> 0%
where the time goes in v1:
time: 472 us; the launch traced here: 465 us
  Pallas kernels  259 us (55%)
  local copies, waits for them, and re-layouts  80.8 us (17%)
  matrix products  71.7 us (15%)
  other arithmetic  51.4 us (11%)
    pallas_call x1, Pallas kernels, scatter_grads(): call(grads_kernel, 'scatter_grads', [jax.ShapeDtypeStruct((BLOB, 128), F3...  77.3 us
    pallas_call x1, Pallas kernels, gather_weights(): call(weights_kernel, 'gather_weights', [jax.ShapeDtypeStruct((2, 4, 4, 2,...  75.9 us
    pallas_call x2, Pallas kernels, scatter_sums(): call(sums_kernel, f'scatter_sums_{number}', [jax.ShapeDtypeStruct((rows,...  38.7 us
    pallas_call x2, Pallas kernels, gather_tokens(): call(tokens_kernel, f'gather_tokens_{number}', [jax.ShapeDtypeStruct((4,...  29.3 us
    dot_general x8, matrix products, matmul(): return jnp.dot(left, right, preferred_element_type=jnp.float32)  24.8 us
    dot_general x8, matrix products, matmul_nt(): lax.dot_general(left, right, (((1,), (1,)), ((), ())), preferred_element_...  21.8 us
    pallas_call x1, Pallas kernels, gather_keys(): call(keys_kernel, 'gather_keys', [jax.ShapeDtypeStruct((2, 4) + key.shape...  19 us
    pallas_call x1, Pallas kernels, scatter_key_grads(): call(key_grads_kernel, 'scatter_key_grads', [jax.ShapeDtypeStruct((rows,...  18.7 us

profile of v1, /device:TPU:0, one launch (start us, length us, event | category | flops | bytes accessed | tf_op | source)
XLA Modules:
  0.0 465.0 jit_solution(16428497295717626737)
XLA Ops:
  2.4 4.1 concatenate.36
  13.1 75.9 %gather_weights.1 = (bf16[2,4,4,2,2,192,128]{6,5,4,3,2,1,0:T(8,128)(2,1)}, bf16[3,4,4,144,432]{4,3,2,1,0:T(8,128)(2,1)}) custom-call(bf16[192,128]{1,0:T(8,128)(2,1)} %maximum_maximum_fusion.1.blob, bf16[3,144,432]{2,1,0:T(8,128)(2,1)} %pad_maximum_fusion.4.ffn), custom_call_target="tpu_custom_call" | custom-call | tf_op jit(solution)/shard_map/gather_weights/pallas_call | solution.py:316
  96.5 4.1 slice.153
  100.7 7.1 %reshape.417 = bf16[1152,1536]{1,0:T(8,128)(2,1)} reshape(bf16[128,108,128]{2,1,0:T(8,128)(2,1)} %slice.153) | data formatting | bytes 7077888 | tf_op jit(solution)/shard_map/reshape | solution.py:744
  107.7 4.8 %reshape.421 = bf16[1024,1152]{1,0:T(8,128)(2,1)S(1)} reshape(bf16[128,72,128]{2,1,0:T(8,128)(2,1)} %slice.163) | data formatting | bytes 4718592 | tf_op jit(solution)/shard_map/reshape | solution.py:745
  120.4 19.0 %gather_keys.1 = (bf16[2,4,128,256]{3,2,1,0:T(8,128)(2,1)}, bf16[2,4,128,256]{3,2,1,0:T(8,128)(2,1)}) custom-call(bf16[128,256]{1,0:T(8,128)(2,1)} %pad_maximum_fusion.15.key, bf16[128,256]{1,0:T(8,128)(2,1)} %slice.217.value), custom_call_target="tpu_custom_call" | custom-call | tf_op jit(solution)/shard_map/gather_keys/pallas_call | solution.py:538
  148.3 13.9 %gather_tokens_5.1 = bf16[4,2,128,1152]{3,2,1,0:T(8,128)(2,1)} custom-call(bf16[128,1152]{1,0:T(8,128)(2,1)} %multiply_convert_fusion.4.own), custom_call_target="tpu_custom_call" | custom-call | tf_op jit(solution)/shard_map/gather_tokens_5/pallas_call | solution.py:646
  162.3 3.5 fusion.39
  175.0 3.5 fusion.1
  178.5 19.3 %scatter_sums_6.1 = f32[128,1152]{1,0:T(8,128)} custom-call(bf16[4,2,128,1152]{3,2,1,0:T(8,128)(2,1)} %bitcast.253), custom_call_target="tpu_custom_call" | custom-call | tf_op jit(solution)/shard_map/scatter_sums_6/pallas_call | solution.py:683
  206.9 15.4 %gather_tokens_7.1 = bf16[4,2,128,1152]{3,2,1,0:T(8,128)(2,1)} custom-call(bf16[128,1152]{1,0:T(8,128)(2,1)} %get-tuple-element.59.own), custom_call_target="tpu_custom_call" | custom-call | tf_op jit(solution)/shard_map/gather_tokens_7/pallas_call | solution.py:646
  222.3 5.9 %multiply_convert_fusion = (bf16[1024,432]{0,1:T(8,128)(2,1)}, bf16[1024,432]{0,1:T(8,128)(2,1)}) fusion(f32[1024,432]{0,1:T(8,128)S(1)} %copy-done.84, f32[1024,432]{0,1:T(8,128)S(1)} %copy-done.85, bf16[1024,1152]{1,0:T(8,128)(2,1)} %bitcast.279, bf16[3,2,1152,432]{3,2,1,0:T(8,128)(2,1)} %bitcast.258), kind=kOutput, calls=%fused_computation.52 | convolution fusion | flops 1029832704 | bytes 8847360 | tf_op jit(solution)/shard_map/dot_general | solution.py:47
  228.2 5.1 %multiply_convert_fusion.1 = (bf16[1024,432]{0,1:T(8,128)(2,1)}, bf16[1024,432]{0,1:T(8,128)(2,1)}) fusion(f32[1024,432]{0,1:T(8,128)S(1)} %copy-done.81, f32[1024,432]{0,1:T(8,128)S(1)} %copy-done.82, bf16[1024,1152]{1,0:T(8,128)(2,1)S(1)} %bitcast.280, bf16[3,2,1152,432]{3,2,1,0:T(8,128)(2,1)} %bitcast.259), kind=kOutput, calls=%fused_computation.53 | convolution fusion | flops 1029832704 | bytes 8847360 | tf_op jit(solution)/shard_map/dot_general | solution.py:47
  237.4 4.1 copy.139
  251.9 4.1 copy.138
  256.0 4.1 copy.137
  260.2 6.8 %pad_maximum_fusion.ffn = bf16[3,4,4,144,432]{4,3,2,1,0:T(8,128)(2,1)} fusion(bf16[1,4,4,144,432]{4,3,2,1,0:T(8,128)(2,1)} %bitcast.249, bf16[1,4,4,144,432]{4,3,2,1,0:T(8,128)(2,1)} %bitcast.250, bf16[1,4,4,144,432]{4,3,2,1,0:T(8,128)(2,1)} %bitcast.251), kind=kLoop, calls=%fused_computation.2 | loop fusion | flops 5971968 | bytes 11943936 | tf_op jit(solution)/shard_map/stack | solution.py:835
  275.9 4.3 fusion.2
  280.3 19.4 %scatter_sums_8.1 = f32[128,1152]{1,0:T(8,128)} custom-call(bf16[4,2,128,1152]{3,2,1,0:T(8,128)(2,1)} %bitcast.252), custom_call_target="tpu_custom_call" | custom-call | tf_op jit(solution)/shard_map/scatter_sums_8/pallas_call | solution.py:683
  315.7 18.7 %scatter_key_grads.1 = (f32[128,256]{1,0:T(8,128)}, f32[128,256]{1,0:T(8,128)}) custom-call(bf16[2,4,128,256]{3,2,1,0:T(8,128)(2,1)} %bitcast.288, bf16[2,4,128,256]{3,2,1,0:T(8,128)(2,1)} %bitcast.287), custom_call_target="tpu_custom_call" | custom-call | tf_op jit(solution)/shard_map/scatter_key_grads/pallas_call | solution.py:594
  361.3 3.6 concatenate.44
  367.3 5.2 %concatenate.41 = bf16[2,4,4,2,2,108,128]{6,5,4,3,2,1,0:T(8,128)(2,1)} reshape(bf16[1152,1536]{1,0:T(8,128)(2,1)S(1)} %convolution_convert_fusion) | data formatting | bytes 7077888 | tf_op jit(solution)/shard_map/concatenate | solution.py:882
  372.5 6.7 %maximum_maximum_fusion.blob = bf16[2,4,4,2,2,192,128]{6,5,4,3,2,1,0:T(8,128)(2,1)} fusion(bf16[2,4,4,2,2,72,128]{6,5,4,3,2,1,0:T(8,128)(2,1)} %concatenate.44, bf16[2,4,4,2,2,4,128]{6,5,4,3,2,1,0:T(4,128)(2,1)} %concatenate.43, bf16[2,4,4,2,2,108,128]{6,5,4,3,2,1,0:T(8,128)(2,1)} %concatenate.41, bf16[192]{0:T(256)(128)(2,1)S(1)} %copy-done.62), kind=kLoop, calls=%fused_computation.3 | loop fusion | flops 25165824 | bytes 12321152 | tf_op jit(solution)/shard_map/concatenate | solution.py:882
  379.2 77.3 %scatter_grads.1 = (f32[192,128]{1,0:T(8,128)}, f32[3,144,432]{2,1,0:T(8,128)}) custom-call(bf16[2,4,4,2,2,192,128]{6,5,4,3,2,1,0:T(8,128)(2,1)} %maximum_maximum_fusion.blob, bf16[3,4,4,144,432]{4,3,2,1,0:T(8,128)(2,1)} %pad_maximum_fusion.ffn), custom_call_target="tpu_custom_call" | custom-call | tf_op jit(solution)/shard_map/scatter_grads/pallas_call | solution.py:485
  (300 shorter events, 126.9 us)
Async XLA Ops:
  2.3 110.2 %copy-start.51 = (f32[128]{0:T(128)}, f32[128]{0:T(128)S(1)}, u32[]{:S(2)}) copy-start(f32[128]{0:T(128)S(1)} %fusion.100) | copy-start | bytes 1540
  2.3 114.0 %copy-start.63 = (f32[128]{0:T(128)}, f32[128]{0:T(128)S(1)}, u32[]{:S(2)}) copy-start(f32[128]{0:T(128)S(1)} %multiply_power_fusion) | copy-start | bytes 1540
  7.2 82.9 %copy-start.61 = (bf16[192]{0:T(256)(128)(2,1)}, bf16[192]{0:T(256)(128)(2,1)S(1)}, u32[]{:S(2)}) copy-start(bf16[192]{0:T(256)(128)(2,1)S(1)} %pad.52.clone) | copy-start | bytes 1156
  8.0 108.3 %copy-start.57 = (f32[128]{0:T(128)}, f32[128]{0:T(128)S(1)}, u32[]{:S(2)}) copy-start(f32[128]{0:T(128)S(1)} %get-tuple-element.46) | copy-start | bytes 1540
  91.1 25.1 %copy-start.42 = (f32[256]{0:T(256)}, f32[256]{0:T(256)S(1)}, u32[]{:S(2)}) copy-start(f32[256]{0:T(256)S(1)} %mul.591) | copy-start | bytes 3076
  117.4 25.1 %copy-start.1 = (f32[128,1024]{1,0:T(8,128)}, f32[128,1024]{1,0:T(8,128)S(1)}, u32[]{:S(2)}) copy-start(f32[128,1024]{1,0:T(8,128)S(1)} %slice.159) | copy-start | bytes 1572868
  118.5 20.9 %copy-start.36 = (pred[128,1024]{0,1:T(8,128)(4,1)S(1)}, pred[128,1024]{0,1:T(8,128)(4,1)}, u32[]{:S(2)}) copy-start(pred[128,1024]{0,1:T(8,128)(4,1)} %broadcast_compare_fusion) | copy-start | bytes 393220
  119.4 23.1 %copy-start.40 = (f32[128,4]{0,1:T(4,128)}, f32[128,4]{0,1:T(4,128)S(1)}, u32[]{:S(2)}) copy-start(f32[128,4]{0,1:T(4,128)S(1)} %copy.116) | copy-start | bytes 6148
  119.4 23.1 %copy-start.38 = (f32[128,4]{0,1:T(4,128)}, f32[128,4]{0,1:T(4,128)S(1)}, u32[]{:S(2)}) copy-start(f32[128,4]{0,1:T(4,128)S(1)} %fusion.99) | copy-start | bytes 6148
  120.4 22.2 %copy-start.32 = (bf16[128,4,128]{2,0,1:T(8,128)(2,1)}, bf16[128,4,128]{2,0,1:T(8,128)(2,1)S(1)}, u32[]{:S(2)}) copy-start(bf16[128,4,128]{2,0,1:T(8,128)(2,1)S(1)} %get-tuple-element.57) | copy-start | bytes 393220
  120.4 22.2 %copy-start.34 = (bf16[128,4,128]{2,0,1:T(8,128)(2,1)}, bf16[128,4,128]{2,0,1:T(8,128)(2,1)S(1)}, u32[]{:S(2)}) copy-start(bf16[128,4,128]{2,0,1:T(8,128)(2,1)S(1)} %get-tuple-element.58) | copy-start | bytes 393220
  178.5 20.6 %copy-start.8 = (bf16[1,128,1152]{2,1,0:T(8,128)(2,1)S(1)}, bf16[1,128,1152]{2,1,0:T(8,128)(2,1)}, u32[]{:S(2)}) copy-start(bf16[1,128,1152]{2,1,0:T(8,128)(2,1)} %param.31) | copy-start | bytes 884740
  178.5 20.6 %copy-start.37 = (f32[1152]{0:T(1024)S(1)}, f32[1152]{0:T(1024)}, u32[]{:S(2)}) copy-start(f32[1152]{0:T(1024)} %mul.644) | copy-start | bytes 13828
  280.3 21.3 %copy-start.69 = (f32[128]{0:T(128)S(1)}, f32[128]{0:T(128)}, u32[]{:S(2)}) copy-start(f32[128]{0:T(128)} %copy-done.68) | copy-start | bytes 1540
  280.3 21.3 %copy-start.9 = (bf16[1,128,1152]{2,1,0:T(8,128)(2,1)S(1)}, bf16[1,128,1152]{2,1,0:T(8,128)(2,1)}, u32[]{:S(2)}) copy-start(bf16[1,128,1152]{2,1,0:T(8,128)(2,1)} %param.31) | copy-start | bytes 884740
  280.3 21.3 %copy-start.50 = (f32[128]{0:T(128)S(1)}, f32[128]{0:T(128)}, u32[]{:S(2)}) copy-start(f32[128]{0:T(128)} %copy-done.49) | copy-start | bytes 1540
  313.5 20.8 %copy-start.58 = (f32[128]{0:T(128)S(1)}, f32[128]{0:T(128)}, u32[]{:S(2)}) copy-start(f32[128]{0:T(128)} %copy-done.57) | copy-start | bytes 1540
  313.5 20.8 %copy-start.64 = (f32[128]{0:T(128)S(1)}, f32[128]{0:T(128)}, u32[]{:S(2)}) copy-start(f32[128]{0:T(128)} %copy-done.63) | copy-start | bytes 1540
  313.5 22.1 %copy-start.43 = (f32[256]{0:T(256)S(1)}, f32[256]{0:T(256)}, u32[]{:S(2)}) copy-start(f32[256]{0:T(256)} %copy-done.42) | copy-start | bytes 3076
  313.5 22.1 %copy-start.54 = (f32[128]{0:T(128)S(1)}, f32[128]{0:T(128)}, u32[]{:S(2)}) copy-start(f32[128]{0:T(128)} %copy-done.53) | copy-start | bytes 1540
  313.5 24.0 %copy-start.73 = (f32[128]{0:T(128)S(1)}, f32[128]{0:T(128)}, u32[]{:S(2)}) copy-start(f32[128]{0:T(128)} %copy-done.72) | copy-start | bytes 1540
  314.8 25.9 %copy-start.39 = (f32[128,4]{0,1:T(4,128)S(1)}, f32[128,4]{0,1:T(4,128)}, u32[]{:S(2)}) copy-start(f32[128,4]{0,1:T(4,128)} %copy-done.38) | copy-start | bytes 6148
  314.8 27.9 %copy-start.41 = (f32[128,4]{0,1:T(4,128)S(1)}, f32[128,4]{0,1:T(4,128)}, u32[]{:S(2)}) copy-start(f32[128,4]{0,1:T(4,128)} %copy-done.40) | copy-start | bytes 6148
  335.6 19.7 %copy-start = (bf16[1152,1536]{1,0:T(8,128)(2,1)S(1)}, bf16[1152,1536]{1,0:T(8,128)(2,1)}, u32[]{:S(2)}) copy-start(bf16[1152,1536]{1,0:T(8,128)(2,1)} %reshape.417) | copy-start | bytes 10616836
  (64 other events, 245.5 us)

commit v2 on v1

--- a/solution.py
+++ b/solution.py
@@ -1,5 +1,3 @@
-from functools import partial
-
 import jax
 import jax.numpy as jnp
 from jax import lax
@@ -609,88 +607,256 @@
     )(keys, values)
 
 
-def tokens_kernel(own, out, send_sems, recv_sems, local_sems):
+class GatherRing:
+    def __init__(self, net, axis, own, place):
+        self.net, self.own, self.place = net, own, place
+        self.mine = net.me[axis]
+        self.left, self.right, self.far = (net.step(axis, by) for by in (3, 1, 2))
+        self.to_left, self.to_right = net.neighbour(axis, 3), net.neighbour(axis, 1)
+
+    def start(self):
+        send, own, place, mine = self.net.send, self.own, self.place, self.mine
+        self.r0 = send(own(0), place(mine, 0), self.to_right)
+        self.l1 = send(own(1), place(mine, 1), self.to_left)
+        self.r1 = send(own(1), place(mine, 1), self.to_right)
+        self.l0 = send(own(0), place(mine, 0), self.to_left)
+
+    def pass_on(self):
+        send, place = self.net.send, self.place
+        self.r0.wait_recv()
+        self.f0 = send(place(self.left, 0), place(self.left, 0), self.to_right)
+        self.l1.wait_recv()
+        self.f1 = send(place(self.right, 1), place(self.right, 1), self.to_left)
+
+    def wait_far(self):
+        self.f0.wait_recv()
+        self.f1.wait_recv()
+
+
+class SumRing:
+    def __init__(self, net, axis, part, bufs):
+        self.net, self.part = net, part
+        self.mine = net.me[axis]
+        self.left, self.right, self.far = (net.step(axis, by) for by in (3, 1, 2))
+        self.to_left, self.to_right = net.neighbour(axis, 3), net.neighbour(axis, 1)
+        self.from_left, self.from_right, self.hold, self.stage = bufs
+
+    def send_far(self):
+        self.a0 = self.net.send(self.part(self.far, 0), self.hold.at[0], self.to_right)
+        self.a1 = self.net.send(self.part(self.far, 1), self.hold.at[1], self.to_left)
+
+    def send_right(self):
+        self.r1 = self.net.send(self.part(self.right, 1), self.from_left.at[1], self.to_right)
+
+    def send_left(self):
+        self.l0 = self.net.send(self.part(self.left, 0), self.from_right.at[0], self.to_left)
+
+    def pass_on(self):
+        self.a0.wait_recv()
+        self.stage[0] = add_up((self.part(self.right, 0), self.hold.at[0])).astype(BF16)
+        self.r0 = self.net.send(self.stage.at[0], self.from_left.at[0], self.to_right)
+        self.a1.wait_recv()
+        self.stage[1] = add_up((self.part(self.left, 1), self.hold.at[1])).astype(BF16)
+        self.l1 = self.net.send(self.stage.at[1], self.from_right.at[1], self.to_left)
+
+    def total(self, h):
+        if h == 0:
+            self.l0.wait_recv()
+            self.r0.wait_recv()
+        else:
+            self.r1.wait_recv()
+            self.l1.wait_recv()
+        return add_up((self.part(self.mine, h), self.from_left.at[h], self.from_right.at[h]))
+
+
+def gelu_parts(u):
+    root = 0.7978845608028654
+    square = u * u
+    th = jnp.tanh(root * u * (1.0 + 0.044715 * square))
+    half = 0.5 * (1.0 + th)
+    slope = half + 0.5 * u * (1.0 - th * th) * (root * (1.0 + 3 * 0.044715 * square))
+    return u * half, slope
+
+
+def ffn_kernel(
+    own,
+    weights,
+    resid,
+    cotangent,
+    gain,
+    outputs,
+    back,
+    gain_grad,
+    weight_grads,
+    send_sems,
+    recv_sems,
+    tokens,
+    grads,
+    act,
+    slope,
+    hidden,
+    gate_g,
+    up_g,
+    branch,
+    *bufs,
+):
     net = Net(send_sems, recv_sems)
     me = net.me
     sibling = net.sibling()
     net.barrier([net.neighbour("y", 1), net.neighbour("y", 3), sibling])
     core, y = me["core"], me["y"]
-    local = pltpu.make_async_copy(own, out.at[y, core], local_sems.at[0])
-    local.start()
-    half = own.shape[0] // 2
-    forwards = [net.send(own, out.at[y, core], sibling)]
+    rows, width = own.shape
+    half = rows // 2
+
+    def cut(h):
+        return pl.ds(h * half, half)
+
+    def phase(source, held, run, bufs, meanwhile):
+        parts, paired, ring_bufs = bufs[0], bufs[1], bufs[2:]
+        gather = GatherRing(
+            net, "y", lambda h: source.at[cut(h)], lambda k, h: held.at[k, core, cut(h)]
+        )
+        gather.start()
+        swap = net.send(source, held.at[y, core], sibling)
+        held[y, core] = source[...]
+        left, right, far = gather.left, gather.right, gather.far
+
+        def across(k):
+            return net.send(held.at[k, core], held.at[k, core], sibling)
+
+        def give(k):
+            return net.send(parts.at[k, 1 - core], paired.at[k], sibling)
+
+        def pair(k, copy):
+            copy.wait_recv()
+            paired[k] = add_up((paired.at[k], parts.at[k, core])).astype(BF16)
+
+        sums = SumRing(net, "y", lambda k, h: paired.at[k, cut(h)], ring_bufs)
+        swap.wait_recv()
+        parts[y] = run(y)
+        pair_own = give(y)
+        gather.pass_on()
+        gather.r1.wait_recv()
+        swap_left = across(left)
+        gather.l0.wait_recv()
+        swap_right = across(right)
+        swap_left.wait_recv()
+        parts[left] = run(left)
+        pair_left = give(left)
+        gather.wait_far()
+        swap_far = across(far)
+        pair(y, pair_own)
+        swap_right.wait_recv()
+        parts[right] = run(right)
+        pair_right = give(right)
+        pair(left, pair_left)
+        sums.send_left()
+        swap_far.wait_recv()
+        parts[far] = run(far)
+        pair_far = give(far)
+        pair(right, pair_right)
+        sums.send_right()
+        pair(far, pair_far)
+        sums.send_far()
+        meanwhile(0)
+        sums.pass_on()
+        meanwhile(1)
+        return sums
+
+    def dot(left, right, dims):
+        return lax.dot_general(left, right, (dims, ((), ())), preferred_element_type=F32)
 
     def forward(k):
-        forwards.append(net.send(out.at[k, core], out.at[k, core], sibling))
-
-    def rows(h):
-        return pl.ds(h * half, half)
-
-    interleave(
-        gather_ring(
-            net,
-            "y",
-            lambda h: own.at[rows(h)],
-            lambda k, h: out.at[k, core, rows(h)],
-            forward,
-        )
-    )
-    for copy in forwards:
-        copy.wait_recv()
-    local.wait()
+        rows_k = tokens[k].reshape(2 * rows, width)
+        total = None
+        for j in range(2):
+            gate = dot(rows_k, weights[0, j], ((1,), (0,)))
+            upper = dot(rows_k, weights[1, j], ((1,), (0,)))
+            value, diff = gelu_parts(gate)
+            act[k, j] = value.astype(BF16)
+            slope[k, j] = (diff * upper).astype(BF16)
+            hidden_low = (value * upper).astype(BF16)
+            hidden[k, j] = hidden_low
+            out = dot(hidden_low, weights[2, j], ((1,), (1,)))
+            total = out if total is None else total + out
+        return total.astype(BF16).reshape(2, rows, width)
+
+    def backward(k):
+        rows_k = grads[k].reshape(2 * rows, width)
+        total = None
+        for j in range(2):
+            hidden_grad = dot(rows_k, weights[2, j], ((1,), (0,)))
+            gate_low = (hidden_grad * slope[k, j].astype(F32)).astype(BF16)
+            up_low = (hidden_grad * act[k, j].astype(F32)).astype(BF16)
+            gate_g[k, j] = gate_low
+            up_g[k, j] = up_low
+            out = dot(gate_low, weights[0, j], ((1,), (1,))) + dot(
+                up_low, weights[1, j], ((1,), (1,))
+            )
+            total = out if total is None else total + out
+        return total.astype(BF16).reshape(2, rows, width)
+
+    def weight_grad(which, held, factor):
+        flat = held[...].reshape(8 * rows, width)
+        for j in range(2):
+            weight_grads[which, j] = dot(
+                flat, factor[:, j].reshape(8 * rows, factor.shape[-1]), ((0,), (0,))
+            ).astype(BF16)
+
+    sums = phase(own, tokens, forward, bufs[:6], lambda step: None)
+    gain_f = gain[...]
+    gain_total = jnp.zeros_like(gain_f)
+    for h in range(2):
+        raw = sums.total(h)
+        upstream = cotangent[cut(h)].astype(F32)
+        scale = lax.rsqrt(jnp.mean(raw * raw, axis=-1, keepdims=True) + EPS)
+        normed = raw * scale
+        outputs[cut(h)] = resid[cut(h)] + normed * gain_f
+        scaled = upstream * gain_f
+        gain_total = gain_total + jnp.sum(upstream * normed, axis=0, keepdims=True)
+        inner = jnp.mean(scaled * normed, axis=-1, keepdims=True)
+        branch[cut(h)] = (scale * (scaled - normed * inner)).astype(BF16)
+    gain_grad[...] = gain_total
+
+    def meanwhile(step):
+        if step == 0:
+            weight_grad(2, grads, hidden)
+        else:
+            weight_grad(0, tokens, gate_g)
+            weight_grad(1, tokens, up_g)
+
+    sums = phase(branch, grads, backward, bufs[6:], meanwhile)
+    for h in range(2):
+        back[cut(h)] = sums.total(h)
     net.send_done()
 
 
-def gather_tokens(own, number):
-    any_ = pl.ANY
+def feed_forward(own, weights, resid, cotangent, gain):
+    rows, width = own.shape
+    wide = weights.shape[-1]
+    vmem = pltpu.VMEM
+    phase_bufs = [
+        pltpu.VMEM((4, 2, rows, width), BF16),
+        pltpu.VMEM((4, rows, width), BF16),
+    ] + [pltpu.VMEM((2, rows // 2, width), BF16)] * 4
     return call(
-        tokens_kernel,
-        f"gather_tokens_{number}",
-        [jax.ShapeDtypeStruct((4, 2) + own.shape, BF16)],
-        [any_],
-        [any_],
-        sems(10) + [pltpu.SemaphoreType.DMA((1,))],
-        number,
-    )(own)[0]
-
-
-def sums_kernel(parts, out, send_sems, recv_sems, paired, *bufs):
-    net = Net(send_sems, recv_sems)
-    me = net.me
-    sibling = net.sibling()
-    net.barrier([net.neighbour("y", 1), net.neighbour("y", 3), sibling])
-    core = me["core"]
-    half = out.shape[0] // 2
-    order = [net.step("y", by) for by in (2, 1, 3)] + [me["y"]]
-    copies = [net.send(parts.at[k, 1 - core], paired.at[k], sibling) for k in order]
-    for k, copy in zip(order, copies):
-        copy.wait_recv()
-        paired[k] = (paired[k].astype(F32) + parts[k, core].astype(F32)).astype(BF16)
-
-    def rows(h):
-        return pl.ds(h * half, half)
-
-    def total(h, terms):
-        out[rows(h)] = add_up(terms)
-
-    interleave(scatter_ring(net, "y", lambda k, h: paired.at[k, rows(h)], bufs, total))
-    net.send_done()
-
-
-def scatter_sums(parts, number):
-    rows, width = parts.shape[2:]
-    vmem = pltpu.VMEM
-    return call(
-        sums_kernel,
-        f"scatter_sums_{number}",
-        [jax.ShapeDtypeStruct((rows, width), F32)],
-        [vmem],
-        [vmem],
-        sems(10)
-        + [pltpu.VMEM((4, rows, width), BF16)]
-        + [pltpu.VMEM((2, rows // 2, width), BF16)] * 4,
-        number,
-    )(parts)[0]
+        ffn_kernel,
+        "feed_forward",
+        [
+            jax.ShapeDtypeStruct((rows, width), F32),
+            jax.ShapeDtypeStruct((rows, width), F32),
+            jax.ShapeDtypeStruct((1, width), F32),
+            jax.ShapeDtypeStruct(weights.shape, BF16),
+        ],
+        [vmem] * 5,
+        [vmem] * 4,
+        sems(40)
+        + [pltpu.VMEM((4, 2, rows, width), BF16)] * 2
+        + [pltpu.VMEM((4, 2, 2 * rows, wide), BF16)] * 5
+        + [pltpu.VMEM((rows, width), BF16)]
+        + phase_bufs * 2,
+        5,
+    )(own, weights, resid, cotangent, gain)
 
 
 def body(
@@ -799,42 +965,11 @@
     resid = hidden_in + post_attn
     normed_mid, mid_back = jax.vjp(rms_norm, resid, gain_ffn)
     ffn_input = normed_mid.astype(jnp.bfloat16)
-    tokens_all = gather_tokens(ffn_input, 5).reshape(-1, width)
-
-    fronts = []
-    partial_out = 0.0
-    for j in range(2):
-        gate_pre = matmul(tokens_all, all_ffn[0, j])
-        up_pre = matmul(tokens_all, all_ffn[1, j])
-        activated, gelu_back = jax.vjp(partial(jax.nn.gelu, approximate=True), gate_pre)
-        hidden_low = (activated * up_pre).astype(jnp.bfloat16)
-        fronts.append((up_pre, activated, gelu_back, hidden_low))
-        partial_out = partial_out + matmul_nt(hidden_low, all_ffn[2, j])
-    branch_raw = scatter_sums(partial_out.astype(BF16).reshape(4, 2, rows, width), 6)
-    post_ffn, post_ffn_back = jax.vjp(rms_norm, branch_raw, gain_branch)
-    outputs = (resid + post_ffn)[None]
+    outputs, grad_ffn_input, grad_gain_branch, ffn_grads = feed_forward(
+        ffn_input, all_ffn, resid, cotangent[0], gain_branch[None]
+    )
+    ffn_grads = ffn_grads.reshape(3, 4, 4, width // 8, ff_own)
     upstream = cotangent[0].astype(jnp.float32)
-    grad_branch, grad_gain_branch = post_ffn_back(upstream)
-    branch_low = grad_branch.astype(jnp.bfloat16)
-    branch_all = gather_tokens(branch_low, 7).reshape(-1, width)
-    grad_tokens_all = 0.0
-    ffn_grads = [[], [], []]
-    for j in range(2):
-        up_pre, activated, gelu_back, hidden_low = fronts[j]
-        grad_hidden = matmul(branch_all, all_ffn[2, j])
-        ffn_grads[2].append(matmul_tn(branch_all, hidden_low))
-        gate_low = gelu_back(grad_hidden * up_pre)[0].astype(jnp.bfloat16)
-        up_low = (grad_hidden * activated).astype(jnp.bfloat16)
-        grad_tokens_all = (
-            grad_tokens_all
-            + matmul_nt(gate_low, all_ffn[0, j])
-            + matmul_nt(up_low, all_ffn[1, j])
-        )
-        ffn_grads[0].append(matmul_tn(tokens_all, gate_low))
-        ffn_grads[1].append(matmul_tn(tokens_all, up_low))
-    ffn_grads = jnp.stack([jnp.stack([g.astype(BF16) for g in pair]) for pair in ffn_grads])
-    ffn_grads = ffn_grads.reshape(3, 4, 4, width // 8, ff_own)
-    grad_ffn_input = scatter_sums(grad_tokens_all.astype(BF16).reshape(4, 2, rows, width), 8)
     grad_resid_mid, grad_gain_ffn = mid_back(grad_ffn_input)
     grad_resid = upstream + grad_resid_mid
     grad_attn_out, grad_gain_mixed = post_attn_back(grad_resid)
@@ -897,7 +1032,7 @@
         gain_sums.append(blob_sum[qkv_rows, at : at + gain.shape[0]])
         at += gain.shape[0]
     return (
-        outputs,
+        outputs[None],
         inputs_grad,
         *gain_sums,
         qkv_sum[:, :qw],

time: 472 us -> 391 us (0.83)
  matrix products: 71.7 us -> 22 us
  local copies, waits for them, and re-layouts: 80.8 us -> 63.3 us
  other arithmetic: 51.4 us -> 34.4 us
    dot_general x8 -> x2, matrix products: 24.8 us -> 3.34 us  [matmul(): return jnp.dot(left, right, preferred_element_type=jnp.float32)]
    dot_general x8 -> x2, matrix products: 21.8 us -> 3.43 us  [matmul_nt(): lax.dot_general(left, right, (((1,), (1,)), ((), ())), preferred_element_...]
    another operation x6 -> x4, local copies, waits for them, and re-layouts: 17.3 us -> 5.74 us  [the longest x3 12.4 us: body(): jnp.stack([g.astype(BF16) for g in pair])]
    another operation x8 -> x4, other arithmetic: 16.6 us -> 6.02 us  [the longest x1 6.78 us: body(): jnp.stack([jnp.stack([g.astype(BF16) for g in pair]) for pair in ffn_grads])]
    dot_general x8 -> x2, matrix products: 13 us -> 3.04 us  [matmul_tn(): lax.dot_general(left, right, (((0,), (0,)), ((), ())), preferred_element_...]
    pallas_call x4 -> x1, Pallas kernels: 68.1 us -> 73.2 us  [feed_forward(): call(ffn_kernel, 'feed_forward', [jax.ShapeDtypeStruct((rows, width), F32...]
    convert_element_type x12 -> x10, local copies, waits for them, and re-layouts: 10.6 us -> 7.65 us  [body(): g.astype(BF16).reshape(n_dev, -1)]
    reduce_sum x5 -> x4, other arithmetic: 9.56 us -> 6.69 us  [rms_norm(): values * lax.rsqrt(jnp.mean(values * values, axis=-1, keepdims=True) + EPS)]
where the time goes in v2:
time: 391 us; the launch traced here: 385 us
  Pallas kernels  263 us (67%)
  local copies, waits for them, and re-layouts  63.3 us (16%)
  other arithmetic  34.4 us (9%)
  matrix products  22 us (6%)
    pallas_call x1, Pallas kernels, scatter_grads(): call(grads_kernel, 'scatter_grads', [jax.ShapeDtypeStruct((BLOB, 128), F3...  77.1 us
    pallas_call x1, Pallas kernels, gather_weights(): call(weights_kernel, 'gather_weights', [jax.ShapeDtypeStruct((2, 4, 4, 2,...  75.9 us
    pallas_call x1, Pallas kernels, feed_forward(): call(ffn_kernel, 'feed_forward', [jax.ShapeDtypeStruct((rows, width), F32...  73.2 us
    pallas_call x1, Pallas kernels, gather_keys(): call(keys_kernel, 'gather_keys', [jax.ShapeDtypeStruct((2, 4) + key.shape...  18.9 us
    pallas_call x1, Pallas kernels, scatter_key_grads(): call(key_grads_kernel, 'scatter_key_grads', [jax.ShapeDtypeStruct((rows,...  18.3 us
    concatenate x3, local copies, waits for them, and re-layouts, body(): jnp.concatenate([grad_qkv_w.astype(BF16).reshape(n_dev, qkv_rows, 128), g...  9.42 us

profile of v2, /device:TPU:0, one launch (start us, length us, event | category | flops | bytes accessed | tf_op | source)
XLA Modules:
  0.0 384.8 jit_solution(2700060908620545976)
XLA Ops:
  2.3 4.1 %concatenate.35 = bf16[40]{0:T(256)(128)(2,1)S(1)} concatenate(bf16[9]{0:T(256)(128)(2,1)} %param.18, bf16[2]{0:T(256)(128)(2,1)} %param.19, bf16[2]{0:T(256)(128)(2,1)} %param.20, bf16[9]{0:T(256)(128)(2,1)} %param.21, bf16[9]{0:T(256)(128)(2,1)} %param.22, bf16[9]{0:T(256)(128)(2,1)} %param.23), dimensions={0} | concatenate | bytes 160 | tf_op jit(solution)/shard_map/concatenate | solution.py:894
  11.2 1.9 pad_maximum_fusion.ffn
  13.1 75.9 %gather_weights.1 = (bf16[2,4,4,2,2,192,128]{6,5,4,3,2,1,0:T(8,128)(2,1)}, bf16[3,4,4,144,432]{4,3,2,1,0:T(8,128)(2,1)}) custom-call(bf16[192,128]{1,0:T(8,128)(2,1)} %maximum_maximum_fusion.1.blob, bf16[3,144,432]{2,1,0:T(8,128)(2,1)} %pad_maximum_fusion.ffn), custom_call_target="tpu_custom_call" | custom-call | tf_op jit(solution)/shard_map/gather_weights/pallas_call | solution.py:314
  92.0 3.3 slice.133
  95.3 4.1 %slice.123 = bf16[128,108,128]{2,1,0:T(8,128)(2,1)} slice(bf16[128,192,128]{2,1,0:T(8,128)(2,1)} %bitcast.174), slice={[0:128], [0:108], [0:128]} | slice | bytes 7077888 | tf_op jit(solution)/shard_map/slice | solution.py:910
  99.4 7.1 %reshape.379 = bf16[1152,1536]{1,0:T(8,128)(2,1)} reshape(bf16[128,108,128]{2,1,0:T(8,128)(2,1)} %slice.123) | data formatting | bytes 7077888 | tf_op jit(solution)/shard_map/reshape | solution.py:910
  106.5 5.1 %reshape.383 = bf16[1024,1152]{1,0:T(8,128)(2,1)S(1)} reshape(bf16[128,72,128]{2,1,0:T(8,128)(2,1)} %slice.133) | data formatting | bytes 4718592 | tf_op jit(solution)/shard_map/reshape | solution.py:911
  111.6 2.7 fusion.35
  119.6 18.9 %gather_keys.1 = (bf16[2,4,128,256]{3,2,1,0:T(8,128)(2,1)}, bf16[2,4,128,256]{3,2,1,0:T(8,128)(2,1)}) custom-call(bf16[128,256]{1,0:T(8,128)(2,1)} %pad_maximum_fusion.11.key, bf16[128,256]{1,0:T(8,128)(2,1)} %slice.163.value), custom_call_target="tpu_custom_call" | custom-call | tf_op jit(solution)/shard_map/gather_keys/pallas_call | solution.py:536
  138.5 3.2 fusion.84
  141.8 2.5 convolution_convert_fusion.3
  146.1 73.2 %feed_forward.1 = (f32[128,1152]{1,0:T(8,128)}, f32[128,1152]{1,0:T(8,128)}, f32[1,1152]{1,0:T(1,128)}, bf16[3,2,1152,432]{3,2,1,0:T(8,128)(2,1)}) custom-call(bf16[128,1152]{1,0:T(8,128)(2,1)} %multiply_convert_fusion.own, bf16[3,2,1152,432]{3,2,1,0:T(8,128)(2,1)} %bitcast.171, f32[128,1152]{1,0:T(8,128)} %copy-done, bf16[128,1152]{1,0:T(8,128)(2,1)} %bitcast.175, ...), custom_call_target="tpu_custom_call" | custom-call | tf_op jit(solution)/shard_map/feed_forward/pallas_call | solution.py:842
  226.9 3.2 fusion.6
  235.0 18.3 %scatter_key_grads.1 = (f32[128,256]{1,0:T(8,128)}, f32[128,256]{1,0:T(8,128)}) custom-call(bf16[2,4,128,256]{3,2,1,0:T(8,128)(2,1)} %bitcast.182, bf16[2,4,128,256]{3,2,1,0:T(8,128)(2,1)} %bitcast.181), custom_call_target="tpu_custom_call" | custom-call | tf_op jit(solution)/shard_map/scatter_key_grads/pallas_call | solution.py:592
  259.4 1.9 multiply_reduce_fusion.6
  261.4 2.1 fusion.29
  263.5 1.8 copy.115
  274.0 2.5 fusion.20
  280.3 3.5 concatenate.43
  283.9 2.3 convolution_convert_fusion
  286.2 5.2 %concatenate.40 = bf16[2,4,4,2,2,108,128]{6,5,4,3,2,1,0:T(8,128)(2,1)} reshape(bf16[1152,1536]{1,0:T(8,128)(2,1)S(1)} %convolution_convert_fusion) | data formatting | bytes 7077888 | tf_op jit(solution)/shard_map/concatenate | solution.py:1017
  291.3 6.8 %maximum_maximum_fusion.blob = bf16[2,4,4,2,2,192,128]{6,5,4,3,2,1,0:T(8,128)(2,1)} fusion(bf16[2,4,4,2,2,72,128]{6,5,4,3,2,1,0:T(8,128)(2,1)} %concatenate.43, bf16[2,4,4,2,2,4,128]{6,5,4,3,2,1,0:T(4,128)(2,1)} %concatenate.42, bf16[2,4,4,2,2,108,128]{6,5,4,3,2,1,0:T(8,128)(2,1)} %concatenate.40, bf16[192]{0:T(256)(128)(2,1)S(1)} %copy-done.30), kind=kLoop, calls=%fused_computation.2 | loop fusion | flops 25165824 | bytes 12321152 | tf_op jit(solution)/shard_map/concatenate | solution.py:1017
  298.1 77.1 %scatter_grads.1 = (f32[192,128]{1,0:T(8,128)}, f32[3,144,432]{2,1,0:T(8,128)}) custom-call(bf16[2,4,4,2,2,192,128]{6,5,4,3,2,1,0:T(8,128)(2,1)} %maximum_maximum_fusion.blob, bf16[3,4,4,144,432]{4,3,2,1,0:T(8,128)(2,1)} %bitcast.170), custom_call_target="tpu_custom_call" | custom-call | tf_op jit(solution)/shard_map/scatter_grads/pallas_call | solution.py:483
  375.2 2.1 slice_bitcast_fusion
  (170 shorter events, 54.2 us)
Async XLA Ops:
  2.3 109.3 %copy-start.23 = (f32[128]{0:T(128)}, f32[128]{0:T(128)S(1)}, u32[]{:S(2)}) copy-start(f32[128]{0:T(128)S(1)} %fusion.66) | copy-start | bytes 1540
  2.3 113.0 %copy-start.31 = (f32[128]{0:T(128)}, f32[128]{0:T(128)S(1)}, u32[]{:S(2)}) copy-start(f32[128]{0:T(128)S(1)} %multiply_power_fusion) | copy-start | bytes 1540
  7.1 82.9 %copy-start.29 = (bf16[192]{0:T(256)(128)(2,1)}, bf16[192]{0:T(256)(128)(2,1)S(1)}, u32[]{:S(2)}) copy-start(bf16[192]{0:T(256)(128)(2,1)S(1)} %pad.43.clone) | copy-start | bytes 1156
  8.0 107.4 %copy-start.27 = (f32[128]{0:T(128)}, f32[128]{0:T(128)S(1)}, u32[]{:S(2)}) copy-start(f32[128]{0:T(128)S(1)} %get-tuple-element.52) | copy-start | bytes 1540
  90.3 28.4 %copy-start.22 = (f32[256]{0:T(256)}, f32[256]{0:T(256)S(1)}, u32[]{:S(2)}) copy-start(f32[256]{0:T(256)S(1)} %mul.454) | copy-start | bytes 3076
  90.5 24.8 %copy-start.17 = (f32[256]{0:T(256)}, f32[256]{0:T(256)S(1)}, u32[]{:S(2)}) copy-start(f32[256]{0:T(256)S(1)} %mul.438) | copy-start | bytes 3076
  106.4 5.1 %copy-start.3 = (bf16[1,128,1152]{2,1,0:T(8,128)(2,1)S(1)}, bf16[1,128,1152]{2,1,0:T(8,128)(2,1)}, u32[]{:S(2)}) copy-start(bf16[1,128,1152]{2,1,0:T(8,128)(2,1)} %param.16) | copy-start | bytes 884740
  114.5 4.3 %copy-start.37 = (f32[128]{0:T(128)}, f32[128]{0:T(128)S(1)}, u32[]{:S(2)}) copy-start(f32[128]{0:T(128)S(1)} %multiply_reduce_fusion.10) | copy-start | bytes 1540
  114.5 4.3 %copy-start.25 = (f32[128]{0:T(128)}, f32[128]{0:T(128)S(1)}, u32[]{:S(2)}) copy-start(f32[128]{0:T(128)S(1)} %fusion.67) | copy-start | bytes 1540
  116.4 25.4 %copy-start.2 = (f32[128,1024]{1,0:T(8,128)}, f32[128,1024]{1,0:T(8,128)S(1)}, u32[]{:S(2)}) copy-start(f32[128,1024]{1,0:T(8,128)S(1)} %slice.129) | copy-start | bytes 1572868
  146.1 75.3 %copy-start.11 = (bf16[1,128,1152]{2,1,0:T(8,128)(2,1)S(1)}, bf16[1,128,1152]{2,1,0:T(8,128)(2,1)}, u32[]{:S(2)}) copy-start(bf16[1,128,1152]{2,1,0:T(8,128)(2,1)} %param.31) | copy-start | bytes 884740
  223.1 3.8 copy-start.15
  226.9 3.2 copy-start.10
  232.9 20.4 %copy-start.28 = (f32[128]{0:T(128)S(1)}, f32[128]{0:T(128)}, u32[]{:S(2)}) copy-start(f32[128]{0:T(128)} %copy-done.27) | copy-start | bytes 1540
  232.9 20.4 %copy-start.32 = (f32[128]{0:T(128)S(1)}, f32[128]{0:T(128)}, u32[]{:S(2)}) copy-start(f32[128]{0:T(128)} %copy-done.31) | copy-start | bytes 1540
  232.9 21.6 %copy-start.18 = (f32[256]{0:T(256)S(1)}, f32[256]{0:T(256)}, u32[]{:S(2)}) copy-start(f32[256]{0:T(256)} %copy-done.17) | copy-start | bytes 3076
  232.9 21.6 %copy-start.26 = (f32[128]{0:T(128)S(1)}, f32[128]{0:T(128)}, u32[]{:S(2)}) copy-start(f32[128]{0:T(128)} %copy-done.25) | copy-start | bytes 1540
  232.9 23.4 %copy-start.38 = (f32[128]{0:T(128)S(1)}, f32[128]{0:T(128)}, u32[]{:S(2)}) copy-start(f32[128]{0:T(128)} %copy-done.37) | copy-start | bytes 1540
  254.5 19.5 %copy-start.1 = (bf16[1152,1536]{1,0:T(8,128)(2,1)S(1)}, bf16[1152,1536]{1,0:T(8,128)(2,1)}, u32[]{:S(2)}) copy-start(bf16[1152,1536]{1,0:T(8,128)(2,1)} %reshape.379) | copy-start | bytes 10616836
  274.0 2.7 copy-start.24
  276.6 3.0 copy-start.9
  276.6 3.0 copy-start.13
  286.2 5.2 %copy-start.30 = (bf16[192]{0:T(256)(128)(2,1)S(1)}, bf16[192]{0:T(256)(128)(2,1)}, u32[]{:S(2)}) copy-start(bf16[192]{0:T(256)(128)(2,1)} %copy-done.29) | copy-start | bytes 1156
  375.2 8.4 %copy-start.14 = (f32[128,1152]{1,0:T(8,128)S(1)}, f32[128,1152]{1,0:T(8,128)}, u32[]{:S(2)}) copy-start(f32[128,1152]{1,0:T(8,128)} %get-tuple-element.31) | copy-start | bytes 1769476
  (15 other events, 22.5 us)
